TPU v7x, 128 devices: a whole 4x4x4 slice. The times are simulated.
128 devices in a mesh: ctx: 16 (over z, x_hi, core), exp: 8 (over y, x_lo).
Axes of the slice: x: 4 (x_hi: 2, x_lo: 2; x = x_hi * 2 + x_lo), y: 4, z: 4, core: 2. Of those that a mesh axis runs over, the one named last changes fastest.
Arguments:
- stream: bfloat16 [2048, 6144], P(('ctx', 'exp')), may hold values from -3 to 3
- queries: bfloat16 [2048, 8192], P('ctx', 'exp'), may hold values from -6 to 6
- key_head_rows: bfloat16 [2048, 1024], P('ctx', 'exp'), may hold values from -6 to 6
- value_head_rows: bfloat16 [2048, 1024], P('ctx', 'exp'), may hold values from -6 to 6
- block_order: int32 [32], replicated, may hold values from 0 to 31, each once
- out_weight: bfloat16 [8192, 6144], P('exp', 'ctx'), may hold values from -0.5 to 0.5
- norm_gain: float32 [6144], replicated, may hold values from 0.5 to 1.5
- gate_weight: bfloat16 [8, 6144, 6144], P('exp', None, 'ctx'), may hold values from -0.078125 to 0.078125
- up_weight: bfloat16 [8, 6144, 6144], P('exp', None, 'ctx'), may hold values from -0.078125 to 0.078125
- down_weight: bfloat16 [8, 6144, 6144], P('exp', 'ctx'), may hold values from -0.078125 to 0.078125
- expert_ids: int32 [2048, 2], P(('ctx', 'exp')), may hold values from 0 to 7, all different within a row; in each aligned block of 16 rows (0 to 15, 16 to 31, ...) at most 8 rows name the same one
- expert_weights: float32 [2048, 2], P(('ctx', 'exp')), may hold values from 0.2 to 1
Outputs:
- attended: bfloat16 [2048, 6144], P(('ctx', 'exp'))
- mixed: bfloat16 [2048, 6144], P(('ctx', 'exp'))
Inputs may be any that keep to these rules, and one draw needn't show every extreme that they name: `expert_ids`: in each aligned block of 16 rows no expert is named by more than 8 rows, a bound that some block reaches; the two experts of a row differ. `block_order`: A permutation of the stored half-blocks of 64 rows.
All inputs are finite; a program needn't handle non-finite values.
Results may differ from a plain program's by a relative error of at most 0.025.
Values may be sent and summed in bfloat16 or wider, within the bound.
A program may use at most 128 MiB of HBM per device.

v0:
```python
import jax
import jax.numpy as jnp
from jax import lax
from jax.sharding import PartitionSpec as P

PER_LANE_DIM = 128


def row_positions(block_order, start, count, half):
    rows = start + jnp.arange(count, dtype=jnp.int32)
    blocks = rows // half
    table = (blocks[:, None] == jnp.arange(block_order.shape[0], dtype=jnp.int32)[None, :]).astype(
        jnp.int32
    )
    first = jnp.sum(table * block_order[None, :], axis=1)
    return first * half + rows % half


def slot_table(ids, experts):
    flat = ids.reshape(-1)
    onehot = (flat[:, None] == jnp.arange(experts, dtype=jnp.int32)[None, :]).astype(jnp.int32)
    earlier_mask = jnp.cumsum(onehot, axis=0) - onehot
    return (flat, jnp.sum(earlier_mask * onehot, axis=1))


def on_device(
    stream,
    queries,
    key_head_rows,
    value_head_rows,
    block_order,
    out_weight,
    norm_gain,
    gate_weight,
    up_weight,
    down_weight,
    expert_ids,
    expert_weights,
):
    n_exp = lax.axis_size("exp")
    block_rows = queries.shape[0]
    half = block_rows // 2
    heads = queries.shape[1] // PER_LANE_DIM
    kv_heads = key_head_rows.shape[1] // PER_LANE_DIM
    head_group = heads // kv_heads
    query_pos = row_positions(block_order, lax.axis_index("ctx") * block_rows, block_rows, half)
    heads_of_query = queries.reshape(block_rows, kv_heads, head_group, PER_LANE_DIM)
    running_max = jnp.full((kv_heads, head_group, block_rows), -1e30, jnp.float32)
    key_piece = lax.all_gather(key_head_rows, "ctx", axis=0, tiled=True)
    value_piece = lax.all_gather(value_head_rows, "ctx", axis=0, tiled=True)
    count = key_piece.shape[0]
    key_pos = row_positions(block_order, jnp.int32(0), count, half)
    heads_of_key = key_piece.reshape(count, kv_heads, PER_LANE_DIM)
    heads_of_value = value_piece.reshape(count, kv_heads, PER_LANE_DIM)
    similarity_logits = jnp.einsum(
        "rkgd,tkd->kgrt", heads_of_query, heads_of_key, preferred_element_type=jnp.float32
    ) * PER_LANE_DIM ** (-0.5)
    visible = key_pos[None, :] <= query_pos[:, None]
    similarity_logits = jnp.where(visible, similarity_logits, -1e30)
    new_max = jnp.maximum(running_max, jnp.max(similarity_logits, axis=-1))
    expd = jnp.where(visible, jnp.exp(similarity_logits - new_max[..., None]), 0.0)
    total = jnp.sum(expd, axis=-1)
    product = jnp.einsum(
        "kgrt,tkd->kgrd",
        expd.astype(jnp.bfloat16),
        heads_of_value,
        preferred_element_type=jnp.float32,
    )
    weighted = product
    running_max, total, weighted = (new_max, total, weighted)
    heads_out = (
        (weighted / total[..., None])
        .transpose(2, 0, 1, 3)
        .reshape(block_rows, heads * PER_LANE_DIM)
        .astype(jnp.bfloat16)
    )
    partial_proj = jnp.dot(
        heads_out,
        lax.all_gather(out_weight, "ctx", axis=1, tiled=True),
        preferred_element_type=jnp.float32,
    )
    moe_rows = stream.shape[0]
    summed_output = lax.psum_scatter(
        partial_proj.astype(jnp.bfloat16), "exp", scatter_dimension=0, tiled=True
    ).astype(jnp.float32)
    attended = (stream.astype(jnp.float32) + summed_output).astype(jnp.bfloat16)
    widened = attended.astype(jnp.float32)
    normed = (
        widened * lax.rsqrt(jnp.mean(widened * widened, axis=-1, keepdims=True) + 1e-05) * norm_gain
    ).astype(jnp.bfloat16)
    capacity = max(2, 4 * moe_rows // n_exp)
    slots_all = n_exp * capacity
    slot_range = jnp.arange(slots_all, dtype=jnp.int32)
    flat, slot = slot_table(expert_ids, n_exp)
    own_target = (flat * capacity + slot).reshape(moe_rows, 2)
    match = jnp.any(own_target[:, :, None] == slot_range[None, None, :], axis=1)
    send = jnp.dot(match.T.astype(jnp.bfloat16), normed, preferred_element_type=jnp.float32).astype(
        jnp.bfloat16
    )
    received = lax.all_to_all(
        send.reshape(n_exp, capacity, send.shape[1]), "exp", split_axis=0, concat_axis=0, tiled=True
    )
    slot_rows = received.reshape(slots_all, send.shape[1])
    gate_local = gate_weight[0]
    up_local = up_weight[0]
    down_local = down_weight[0]
    piece = lax.all_gather(slot_rows, "ctx", axis=0, tiled=True)
    gate_part = jnp.dot(piece, gate_local, preferred_element_type=jnp.float32)
    up_part = jnp.dot(piece, up_local, preferred_element_type=jnp.float32)
    hidden = (jax.nn.silu(gate_part) * up_part).astype(jnp.bfloat16)
    expert_out = lax.psum_scatter(
        jnp.dot(hidden, down_local, preferred_element_type=jnp.float32).astype(jnp.bfloat16),
        "ctx",
        scatter_dimension=0,
        tiled=True,
    )
    back = lax.all_to_all(
        expert_out.reshape(n_exp, capacity, expert_out.shape[1]),
        "exp",
        split_axis=0,
        concat_axis=0,
        tiled=True,
    )
    back = back.reshape(slots_all, expert_out.shape[1])
    combine = jnp.sum(
        jnp.where(
            own_target[:, :, None] == slot_range[None, None, :], expert_weights[:, :, None], 0.0
        ),
        axis=1,
    )
    mixed_wide = widened + jnp.dot(
        combine, back.astype(jnp.float32), precision=lax.Precision.HIGHEST
    )
    return (attended, mixed_wide.astype(jnp.bfloat16))


def solution(mesh):
    in_specs = (
        P(("ctx", "exp"), None),
        P("ctx", "exp"),
        P("ctx", "exp"),
        P("ctx", "exp"),
        P(),
        P("exp", "ctx"),
        P(),
        P("exp", None, "ctx"),
        P("exp", None, "ctx"),
        P("exp", "ctx", None),
        P(("ctx", "exp"), None),
        P(("ctx", "exp"), None),
    )
    out_specs = (P(("ctx", "exp"), None), P(("ctx", "exp"), None))
    return jax.shard_map(
        on_device, mesh=mesh, in_specs=in_specs, out_specs=out_specs, check_vma=False
    )
```

profile of v0, /device:TPU:1, one launch (start us, length us, event | category | flops | bytes accessed | tf_op | source)
XLA Modules:
  0.0 441.6 jit_solution(17704466567746694739)
XLA Ops:
  7.2 0.0 copy-start
  7.2 0.0 all-gather.3.cloned.1.call-start
  7.2 0.7 all-gather.3.cloned.1.call-update
  7.9 0.0 reduce-scatter.3.cloned.1.call-start
  8.0 0.9 copy.36
  8.9 0.7 select_reduce_fusion.3
  9.6 0.8 select_reduce_fusion
  10.4 31.1 %all_gather.12 = bf16[2048,128]{1,0:T(8,128)(2,1)S(1)} all-gather(bf16[128,128]{1,0:T(8,128)(2,1)} %param.14), channel_id=1, replica_groups=mesh['ctx'=16,'exp'=8] {'ctx'}, dimensions={0}, use_global_device_ids=true | all-gather | bytes 557056 | tf_op jit(solution)/shard_map/all_gather | solution.py:49
  41.5 0.3 broadcast_compare_fusion
  41.9 0.0 copy-done
  41.9 1.4 fusion
  43.2 21.7 %all_gather.13 = bf16[2048,128]{0,1:T(8,128)(2,1)S(1)} all-gather(bf16[128,128]{0,1:T(8,128)(2,1)S(1)} %copy.36), channel_id=1, replica_groups=mesh['ctx'=16,'exp'=8] {'ctx'}, dimensions={0}, use_global_device_ids=true | all-gather | bytes 557056 | tf_op jit(solution)/shard_map/all_gather | solution.py:50
  65.0 2.0 fusion.3
  67.0 2.2 fusion.23
  69.2 45.3 %all-gather.3.cloned.1.call-done = bf16[1024,6144]{1,0:T(8,128)(2,1)} async-done(((bf16[1024,384]{1,0:T(8,128)(2,1)}), bf16[1024,6144]{1,0:T(8,128)(2,1)}) %all-gather.3.cloned.1.call-update) | async-done | bytes 12582928 | tf_op jit(solution)/shard_map/all_gather | solution.py:79
  114.6 0.0 copy-start.5
  114.6 0.0 copy-start.3
  114.6 0.0 copy-start.4
  114.6 7.7 %convolution_convert_fusion.1 = bf16[128,6144]{1,0:T(8,128)(2,1)} fusion(bf16[128,1024]{0,1:T(8,128)(2,1)S(1)} %bitcast.77, bf16[1024,6144]{1,0:T(8,128)(2,1)} %all-gather.3.cloned.1.call-done), kind=kOutput, calls=%fused_computation.4 | convolution fusion | flops 1611399168 | bytes 14417920 | tf_op jit(solution)/shard_map/dot_general | solution.py:77
  122.3 0.0 reduce-scatter.3.cloned.1.call-update
  122.3 0.0 all-gather.5.cloned.1.call-start
  122.3 0.0 copy-done.5
  122.3 0.1 copy.38
  122.4 0.1 eq.36
  122.5 0.1 fusion.39
  122.6 0.1 reduce_window_sum.11
  122.6 0.2 select_reduce_fusion.2
  122.8 0.1 reduce_sum.60
  122.9 0.1 copy.39
  123.0 0.1 fusion.38
  123.1 37.0 %reduce-scatter.3.cloned.1.call-done = bf16[16,6144]{1,0:T(8,128)(2,1)} async-done(((bf16[128,6144]{1,0:T(8,128)(2,1)}), bf16[16,6144]{1,0:T(8,128)(2,1)}) %reduce-scatter.3.cloned.1.call-update) | async-done | bytes 196624 | tf_op jit(solution)/shard_map/reduce_scatter | solution.py:83
  160.1 0.0 copy-done.3
  160.1 1.1 fusion.30
  161.2 0.0 copy-start.2
  161.2 0.0 copy-done.4
  161.2 0.4 fusion.1
  161.6 13.2 %all_to_all.10 = bf16[8,8,6144]{2,1,0:T(8,128)(2,1)} all-to-all(bf16[8,8,6144]{2,1,0:T(8,128)(2,1)S(1)} %fusion.1), channel_id=1, replica_groups=mesh['ctx'=16,'exp'=8] {'exp'}, dimensions={0} | all-to-all | bytes 1572864 | tf_op jit(solution)/shard_map/all_to_all | solution.py:100
  174.8 0.0 all-gather.5.cloned.1.call-update
  174.8 0.2 reduce-scatter.5.cloned.1.call-start
  175.0 94.5 %all-gather.5.cloned.1.call-done = bf16[1024,6144]{1,0:T(8,128)(2,1)} async-done(((bf16[64,6144]{1,0:T(8,128)(2,1)}), bf16[1024,6144]{1,0:T(8,128)(2,1)}) %all-gather.5.cloned.1.call-update) | async-done | bytes 12582928 | tf_op jit(solution)/shard_map/all_gather | solution.py:107
  269.6 0.0 copy-start.7
  269.6 0.0 slice-start
  269.6 11.1 %fusion.8 = f32[1024,384]{1,0:T(8,128)S(1)} fusion(bf16[1024,6144]{1,0:T(8,128)(2,1)} %all-gather.5.cloned.1.call-done, bf16[1,6144,384]{2,1,0:T(8,128)(2,1)} %param.19), kind=kOutput, calls=%fused_computation.14 | convolution fusion | flops 4831838208 | bytes 18874368 | tf_op jit(solution)/shard_map/dot_general | solution.py:108
  280.7 0.0 copy-done.7
  280.7 0.0 slice-start.1
  280.7 8.9 %fusion.17 = bf16[1024,384]{1,0:T(8,128)(2,1)S(1)} fusion(bf16[1024,6144]{1,0:T(8,128)(2,1)S(1)} %copy-done.7, bf16[1,6144,384]{2,1,0:T(8,128)(2,1)} %param.20, f32[1024,384]{1,0:T(8,128)S(1)} %fusion.8), kind=kOutput, calls=%fused_computation.20 | convolution fusion | flops 4834197504 | bytes 19660800 | tf_op jit(solution)/shard_map/dot_general | solution.py:109
  289.7 0.0 slice-done
  289.7 0.0 slice-done.1
  289.7 0.0 copy-start.1
  289.7 9.6 %convolution_convert_fusion = bf16[1024,6144]{1,0:T(8,128)(2,1)} fusion(bf16[1024,384]{1,0:T(8,128)(2,1)S(1)} %fusion.17, bf16[1,384,6144]{2,1,0:T(8,128)(2,1)S(1)} %bitcast.79), kind=kOutput, calls=%fused_computation | convolution fusion | flops 4838129664 | bytes 18087936 | tf_op jit(solution)/shard_map/dot_general | solution.py:112
  299.3 0.0 copy-start.6
  299.3 0.0 reduce-scatter.5.cloned.1.call-update
  299.3 119.2 %reduce-scatter.5.cloned.1.call-done = bf16[64,6144]{1,0:T(8,128)(2,1)} async-done(((bf16[1024,6144]{1,0:T(8,128)(2,1)}), bf16[64,6144]{1,0:T(8,128)(2,1)}) %reduce-scatter.5.cloned.1.call-update) | async-done | bytes 786448 | tf_op jit(solution)/shard_map/reduce_scatter | solution.py:111
  418.6 4.0 all-to-all-start.1
  422.6 0.0 copy-done.6
  422.6 0.1 select_reduce_fusion.1
  422.7 11.3 %all-to-all-done.1 = bf16[8,8,6144]{2,1,0:T(8,128)(2,1)S(1)} async-done(((bf16[8,8,6144]{2,1,0:T(8,128)(2,1)}), bf16[8,8,6144]{2,1,0:T(8,128)(2,1)S(1)}, u32[]{:S(2)}, u32[]{:S(2)}) %all-to-all-start.1) | async-done | bytes 786464 | tf_op jit(solution)/shard_map/all_to_all | solution.py:117
  434.0 0.0 copy-done.2
  434.0 1.1 fusion.2
  435.1 0.0 copy-done.1
  (8 shorter events, 0.0 us)
Async XLA Ops:
  7.2 34.7 %copy-start = (bf16[128,1024]{1,0:T(8,128)(2,1)S(1)}, bf16[128,1024]{1,0:T(8,128)(2,1)}, u32[]{:S(2)}) copy-start(bf16[128,1024]{1,0:T(8,128)(2,1)} %param.13) | copy-start | bytes 786436
  7.2 107.4 %all-gather.3.cloned.1.call-start = ((), (), s32[]{:S(2)}) async-start(), calls=%async_computation.4 | async-start | bytes 13369344 | tf_op jit(solution)/shard_map/all_gather | solution.py:79
  7.9 152.1 %reduce-scatter.3.cloned.1.call-start = ((), (), s32[]{:S(2)}) async-start(), calls=%async_computation.5 | async-start | bytes 1769472 | tf_op jit(solution)/shard_map/reduce_scatter | solution.py:83
  114.6 7.8 %copy-start.5 = (s32[16,2]{0,1:T(2,128)S(1)}, s32[16,2]{0,1:T(2,128)}, u32[]{:S(2)}) copy-start(s32[16,2]{0,1:T(2,128)} %param.22) | copy-start | bytes 388
  114.6 45.5 %copy-start.3 = (bf16[16,6144]{1,0:T(8,128)(2,1)S(1)}, bf16[16,6144]{1,0:T(8,128)(2,1)}, u32[]{:S(2)}) copy-start(bf16[16,6144]{1,0:T(8,128)(2,1)} %param.12) | copy-start | bytes 589828
  114.6 46.6 %copy-start.4 = (f32[6144]{0:T(1024)S(1)}, f32[6144]{0:T(1024)}, u32[]{:S(2)}) copy-start(f32[6144]{0:T(1024)} %param.18) | copy-start | bytes 73732
  122.3 147.3 %all-gather.5.cloned.1.call-start = ((), (), s32[]{:S(2)}) async-start(), calls=%async_computation.6 | async-start | bytes 13369344 | tf_op jit(solution)/shard_map/all_gather | solution.py:107
  161.2 272.8 %copy-start.2 = (bf16[16,6144]{1,0:T(8,128)(2,1)}, bf16[16,6144]{1,0:T(8,128)(2,1)S(1)}, u32[]{:S(2)}) copy-start(bf16[16,6144]{1,0:T(8,128)(2,1)S(1)} %get-tuple-element.3) | copy-start | bytes 589828
  174.8 243.7 %reduce-scatter.5.cloned.1.call-start = ((), (), s32[]{:S(2)}) async-start(), calls=%async_computation.7 | async-start | bytes 13369344 | tf_op jit(solution)/shard_map/reduce_scatter | solution.py:111
  269.6 11.1 %copy-start.7 = (bf16[1024,6144]{1,0:T(8,128)(2,1)S(1)}, bf16[1024,6144]{1,0:T(8,128)(2,1)}, u32[]{:S(2)}) copy-start(bf16[1024,6144]{1,0:T(8,128)(2,1)} %all-gather.5.cloned.1.call-done) | copy-start | bytes 37748740
  269.6 20.1 %slice-start = ((s8[4718592]{0:T(1024)(128)(4,1)}), s8[4194304]{0:T(1024)(128)(4,1)S(1)}, s32[]{:S(2)}) async-start(s8[4718592]{0:T(1024)(128)(4,1)} %bitcast.78), calls=%async_computation.8 | async-start | bytes 8388608
  280.7 9.0 %slice-start.1 = ((s8[4718592]{0:T(1024)(128)(4,1)}), s8[524288]{0:T(1024)(128)(4,1)S(1)}, s32[]{:S(2)}) async-start(s8[4718592]{0:T(1024)(128)(4,1)} %bitcast.78), calls=%async_computation.9 | async-start | bytes 1048576
  289.7 145.4 %copy-start.1 = (bf16[128,1024]{1,0:T(8,128)(2,1)S(1)}, bf16[128,1024]{1,0:T(8,128)(2,1)}, u32[]{:S(2)}) copy-start(bf16[128,1024]{1,0:T(8,128)(2,1)} %param.13) | copy-start | bytes 786436
  299.3 123.3 %copy-start.6 = (f32[16,2]{0,1:T(2,128)S(1)}, f32[16,2]{0,1:T(2,128)}, u32[]{:S(2)}) copy-start(f32[16,2]{0,1:T(2,128)} %param.23) | copy-start | bytes 388
  418.6 15.4 %all-to-all-start.1 = ((bf16[8,8,6144]{2,1,0:T(8,128)(2,1)}), bf16[8,8,6144]{2,1,0:T(8,128)(2,1)S(1)}, u32[]{:S(2)}, u32[]{:S(2)}) async-start(bf16[8,8,6144]{2,1,0:T(8,128)(2,1)} %bitcast.76), calls=%async_computation.3 | async-start | bytes 1572864 | tf_op jit(solution)/shard_map/all_to_all | solution.py:117
Sparse Core Ops, SparseCore 0:
  10.4 104.1 all-gather.2
  122.4 37.6 reduce-scatter.2
  174.9 94.5 all-gather.4
  299.4 119.0 reduce-scatter.4
where the time goes:
time: 443 us; the launch traced here: 442 us
  waiting for transfers between devices  308 us (70%)
  blocking collectives  66 us (15%)
  matrix products  42.4 us (10%)
  between operations  14 us (3%)
  other arithmetic  5.48 us (1%)
    reduce_scatter x1, waiting for transfers between devices, on_device(): lax.psum_scatter(jnp.dot(hidden, down_local, preferred_element_type=jnp.f...  119 us
    all_gather x1, waiting for transfers between devices, on_device(): piece = lax.all_gather(slot_rows, 'ctx', axis=0, tiled=True)  94.5 us
    all_gather x1, waiting for transfers between devices, on_device(): lax.all_gather(out_weight, 'ctx', axis=1, tiled=True)  45.3 us
    reduce_scatter x1, waiting for transfers between devices, on_device(): lax.psum_scatter(partial_proj.astype(jnp.bfloat16), 'exp', scatter_dimens...  37 us
    all_gather x1, blocking collectives, on_device(): key_piece = lax.all_gather(key_head_rows, 'ctx', axis=0, tiled=True)  31.1 us
    all_gather x1, blocking collectives, on_device(): value_piece = lax.all_gather(value_head_rows, 'ctx', axis=0, tiled=True)  21.7 us
    all_to_all x1, blocking collectives, on_device(): lax.all_to_all(send.reshape(n_exp, capacity, send.shape[1]), 'exp', split...  13.2 us
    all_to_all x1, waiting for transfers between devices, on_device(): lax.all_to_all(expert_out.reshape(n_exp, capacity, expert_out.shape[1]),...  11.3 us
  transfers between devices with their start and end apart: 5, of which 5 were waited for; matrix products, arithmetic and copies ran while one was open for 2% of the time, Pallas kernels for 0%

commit v1 on v0

--- a/solution.py
+++ b/solution.py
@@ -1,9 +1,409 @@
+import functools
+
 import jax
 import jax.numpy as jnp
 from jax import lax
+from jax.experimental import pallas as pl
+from jax.experimental.pallas import tpu as pltpu
 from jax.sharding import PartitionSpec as P
 
 PER_LANE_DIM = 128
+MESH = pl.DeviceIdType.MESH
+VMEM_LIMIT = 60 * 2**20
+NC = 4
+
+
+def place():
+    ctx = lax.axis_index("ctx")
+    exp = lax.axis_index("exp")
+    return ctx // 4, lax.rem(ctx // 2, 2), lax.rem(ctx, 2), exp
+
+
+def remote(src, dst, send, recv, device):
+    return pltpu.make_async_remote_copy(
+        src_ref=src, dst_ref=dst, send_sem=send, recv_sem=recv, device_id=device, device_id_type=MESH
+    )
+
+
+def greet(devices):
+    barrier = pltpu.get_barrier_semaphore()
+    for device in devices:
+        pl.semaphore_signal(barrier, inc=1, device_id=device, device_id_type=MESH)
+    pl.semaphore_wait(barrier, len(devices))
+
+
+def slot_match(meta, core):
+    row = lax.broadcasted_iota(jnp.int32, (128, 128), 0)
+    lane = lax.broadcasted_iota(jnp.int32, (128, 128), 1)
+    expert = (row // 16).astype(jnp.float32)
+    first = (meta[0:1, :] == expert) & (lane < 16)
+    second = (meta[1:2, :] == expert) & (lane < 16)
+    named = jnp.where(first | second, 1.0, 0.0)
+    earlier = jnp.where(row < lane, 1.0, 0.0)
+    rank = jnp.dot(
+        named.astype(jnp.bfloat16), earlier.astype(jnp.bfloat16), preferred_element_type=jnp.float32
+    )
+    slot = lax.rem(row, 8).astype(jnp.float32)
+    mine = lax.rem(row // 8, 2) == core
+    match = jnp.where((rank == slot) & mine, named, 0.0)
+    weight = match * jnp.where(first, meta[2:3, :], meta[3:4, :])
+    return match[:, :16].astype(jnp.bfloat16), weight.T[:16, :]
+
+
+def experts_kernel(
+    att_ref, gain_ref, meta_ref, gate_ref, up_ref, down_ref, out_ref,
+    wgu, wd, meta_sib, nrm, nsib, disp, rows, rows_sib, acc, hid, part,
+    got1, got2, got3, got4, got5, final, back, contrib, contrib_sib,
+    load_sem, pre_s, pre_r, disp_s, disp_r, ga_s, ga_r, sib_s, sib_r, hid_s, hid_r, rs_s, rs_r, back_s, back_r,
+):
+    z, xh, core, exp = place()
+    width = rows.shape[-1]
+    half = NC * width
+    up_z, down_z, far_z = lax.rem(z + 1, 4), lax.rem(z + 3, 4), lax.rem(z + 2, 4)
+
+    def dev(a, b, c=None, e=None):
+        return (a * 4 + b * 2 + (core if c is None else c), exp if e is None else e)
+
+    def blk(a, b):
+        return a * 2 + b
+
+    zp, zm, xp, sib = dev(up_z, xh), dev(down_z, xh), dev(z, 1 - xh), dev(z, xh, 1 - core)
+    peers = [lax.rem(exp + j, 8) for j in range(1, 8)]
+    own_block = blk(z, xh)
+
+    loads = [
+        pltpu.make_async_copy(gate_ref.at[0], wgu.at[:, pl.ds(0, 384)], load_sem.at[0]),
+        pltpu.make_async_copy(up_ref.at[0], wgu.at[:, pl.ds(384, 384)], load_sem.at[1]),
+        pltpu.make_async_copy(
+            down_ref.at[0, :, pl.ds(pl.multiple_of(core * half, 128), half)],
+            wd.at[pl.ds(pl.multiple_of(core * 384, 128), 384)],
+            load_sem.at[2],
+        ),
+    ]
+    for load in loads:
+        load.start()
+    greet([zp, zm, xp, sib] + [dev(z, xh, None, e) for e in peers])
+
+    send_meta = remote(meta_ref, meta_sib, pre_s.at[0], pre_r.at[0], sib)
+    send_meta.start()
+    wide = att_ref[...].astype(jnp.float32)
+    normed = (
+        wide * lax.rsqrt(jnp.mean(wide * wide, axis=-1, keepdims=True) + 1e-05) * gain_ref[...]
+    ).astype(jnp.bfloat16)
+    nrm[0] = normed[:, :half]
+    nrm[1] = normed[:, half:]
+    send_nrm = remote(nrm.at[1 - core], nsib, pre_s.at[1], pre_r.at[1], sib)
+    send_nrm.start()
+    match_own, weight_own = slot_match(meta_ref[...], core)
+    send_meta.wait_recv()
+    match_sib, weight_sib = slot_match(meta_sib[...], 1 - core)
+    send_nrm.wait_recv()
+
+    dispatches = []
+    for c in range(NC):
+        cols = pl.ds(c * width, width)
+        picked = jnp.dot(match_own, nrm[core, :, cols], preferred_element_type=jnp.float32) + jnp.dot(
+            match_sib, nsib[:, cols], preferred_element_type=jnp.float32
+        )
+        disp[c] = picked.astype(jnp.bfloat16).reshape(8, 16, width)
+        sends = []
+        for j, e in enumerate(peers):
+            copy = remote(
+                disp.at[c, e], rows.at[c, own_block, exp], disp_s.at[c, j], disp_r.at[c, j],
+                dev(z, xh, None, e),
+            )
+            copy.start()
+            sends.append(copy)
+        rows[c, own_block, exp] = disp[c, exp]
+        dispatches.append(sends)
+    send_down = remote(
+        down_ref.at[0, :, pl.ds(pl.multiple_of((1 - core) * half, 128), half)],
+        wd.at[pl.ds(pl.multiple_of(core * 384, 128), 384)],
+        pre_s.at[2], pre_r.at[2], sib,
+    )
+    send_down.start()
+
+    gather = [[None] * 8 for _ in range(NC)]
+    shares = [[] for _ in range(NC)]
+
+    def forward(c, k, block, device, part_of=None):
+        ref = rows.at[c, block] if part_of is None else rows.at[c, block, pl.ds(part_of * 4, 4)]
+        gather[c][k] = remote(ref, ref, ga_s.at[c, k], ga_r.at[c, k], device)
+        gather[c][k].start()
+
+    def share(c, block):
+        j = len(shares[c])
+        copy = remote(rows.at[c, block], rows_sib.at[c, block], sib_s.at[c, j], sib_r.at[c, j], sib)
+        copy.start()
+        shares[c].append(copy)
+
+    def gather_a(c):
+        for copy in dispatches[c]:
+            copy.wait_recv()
+        forward(c, 0, own_block, zp)
+        forward(c, 1, own_block, zm)
+        forward(c, 2, own_block, xp)
+        share(c, own_block)
+
+    def gather_b(c):
+        gather[c][0].wait_recv()
+        forward(c, 3, blk(down_z, xh), zp, 0)
+        share(c, blk(down_z, xh))
+        gather[c][1].wait_recv()
+        forward(c, 4, blk(up_z, xh), zm, 1)
+        share(c, blk(up_z, xh))
+        gather[c][2].wait_recv()
+        forward(c, 5, blk(z, 1 - xh), zp)
+        forward(c, 6, blk(z, 1 - xh), zm)
+        share(c, blk(z, 1 - xh))
+
+    def gather_c(c):
+        gather[c][3].wait_recv()
+        gather[c][4].wait_recv()
+        forward(c, 7, blk(far_z, xh), xp)
+        share(c, blk(far_z, xh))
+
+    def gather_d(c):
+        gather[c][5].wait_recv()
+        share(c, blk(down_z, 1 - xh))
+        gather[c][6].wait_recv()
+        share(c, blk(up_z, 1 - xh))
+        gather[c][7].wait_recv()
+        share(c, blk(far_z, 1 - xh))
+
+    def multiply(source, c, first_col, fresh):
+        base = pl.multiple_of(first_col + c * width, 128)
+
+        def body(i, carry):
+            lhs = source[c, pl.ds(i * 2, 2)].reshape(256, width)
+            term = jnp.dot(lhs, wgu[pl.ds(base, width), :], preferred_element_type=jnp.float32)
+            if fresh:
+                acc[i] = term
+            else:
+                acc[i] += term
+            return carry
+
+        lax.fori_loop(0, 4, body, 0)
+
+    def multiply_own(c):
+        if c == 0:
+            loads[0].wait()
+            loads[1].wait()
+        multiply(rows, c, core * half, c == 0)
+
+    def multiply_sib(c):
+        for copy in shares[c]:
+            copy.wait_recv()
+        multiply(rows_sib, c, (1 - core) * half, False)
+
+    gather_a(0)
+    gather_a(1)
+    gather_b(0)
+    gather_c(0)
+    gather_a(2)
+    gather_b(1)
+    gather_d(0)
+    multiply_own(0)
+    gather_c(1)
+    gather_a(3)
+    gather_b(2)
+    gather_d(1)
+    multiply_sib(0)
+    gather_c(2)
+    multiply_own(1)
+    gather_b(3)
+    gather_d(2)
+    multiply_sib(1)
+    gather_c(3)
+    multiply_own(2)
+    multiply_sib(2)
+    gather_d(3)
+    multiply_own(3)
+    multiply_sib(3)
+
+    mine = pl.ds(pl.multiple_of(core * 384, 128), 384)
+    sent_hidden = []
+    for i in range(4):
+        gate_part = acc[i, :, :384]
+        up_part = acc[i, :, 384:]
+        hid[i, :, mine] = (gate_part / (1.0 + jnp.exp(-gate_part)) * up_part).astype(jnp.bfloat16)
+        copy = remote(hid.at[i, :, mine], hid.at[i, :, mine], hid_s.at[i], hid_r.at[i], sib)
+        copy.start()
+        sent_hidden.append(copy)
+    loads[2].wait()
+    send_down.wait_recv()
+    for copy in sent_hidden:
+        copy.wait_recv()
+
+    reduce = [[None] * 8 for _ in range(NC)]
+    returns = []
+
+    def send_sum(c, k, src, dst, device):
+        reduce[c][k] = remote(src, dst, rs_s.at[c, k], rs_r.at[c, k], device)
+        reduce[c][k].start()
+
+    def f32(value):
+        return value.astype(jnp.float32)
+
+    def reduce_a(c):
+        def body(i, carry):
+            out = jnp.dot(hid[i], wd[:, c * width : (c + 1) * width], preferred_element_type=jnp.float32)
+            part[c, pl.ds(i * 2, 2)] = out.astype(jnp.bfloat16).reshape(2, 8, 16, width)
+            return carry
+
+        lax.fori_loop(0, 4, body, 0)
+        send_sum(c, 0, part.at[c, blk(up_z, 1 - xh)], got1.at[c, 0], zp)
+        send_sum(c, 1, part.at[c, blk(down_z, 1 - xh)], got1.at[c, 1], zm)
+        send_sum(c, 2, part.at[c, blk(far_z, 1 - xh)], got2.at[c], xp)
+
+    def reduce_b(c):
+        reduce[c][2].wait_recv()
+        block = blk(far_z, xh)
+        part[c, block] = (f32(part[c, block]) + f32(got2[c])).astype(jnp.bfloat16)
+        send_sum(c, 3, part.at[c, block, pl.ds(0, 4)], got4.at[c, 0], zm)
+        send_sum(c, 4, part.at[c, block, pl.ds(4, 4)], got4.at[c, 1], zp)
+        reduce[c][0].wait_recv()
+        reduce[c][1].wait_recv()
+        block = blk(z, 1 - xh)
+        part[c, block] = (f32(part[c, block]) + f32(got1[c, 0]) + f32(got1[c, 1])).astype(jnp.bfloat16)
+        send_sum(c, 5, part.at[c, block], got3.at[c], xp)
+
+    def reduce_c(c):
+        reduce[c][3].wait_recv()
+        block = blk(down_z, xh)
+        part[c, block, 0:4] = (f32(part[c, block, 0:4]) + f32(got4[c, 0])).astype(jnp.bfloat16)
+        send_sum(c, 6, part.at[c, block], got5.at[c, 0], zm)
+        reduce[c][4].wait_recv()
+        block = blk(up_z, xh)
+        part[c, block, 4:8] = (f32(part[c, block, 4:8]) + f32(got4[c, 1])).astype(jnp.bfloat16)
+        send_sum(c, 7, part.at[c, block], got5.at[c, 1], zp)
+
+    def reduce_d(c):
+        reduce[c][5].wait_recv()
+        reduce[c][6].wait_recv()
+        reduce[c][7].wait_recv()
+        final[c] = (
+            f32(part[c, own_block]) + f32(got3[c]) + (f32(got5[c, 0]) + f32(got5[c, 1]))
+        ).astype(jnp.bfloat16)
+        sends = []
+        for j, e in enumerate(peers):
+            copy = remote(
+                final.at[c, e], back.at[c, exp], back_s.at[c, j], back_r.at[c, j], dev(z, xh, None, e)
+            )
+            copy.start()
+            sends.append(copy)
+        back[c, exp] = final[c, exp]
+        returns.append(sends)
+
+    def combine(c):
+        for copy in returns[c]:
+            copy.wait_recv()
+        values = f32(back[c].reshape(128, width))
+        contrib_sib[:, c * width : (c + 1) * width] = jnp.dot(
+            weight_sib, values, precision=lax.Precision.HIGHEST, preferred_element_type=jnp.float32
+        )
+        total = jnp.dot(
+            weight_own, values, precision=lax.Precision.HIGHEST, preferred_element_type=jnp.float32
+        )
+        cols = pl.ds(pl.multiple_of(core * half + c * width, 128), width)
+        out_ref[:, cols] = (f32(att_ref[:, cols]) + total).astype(jnp.bfloat16)
+
+    reduce_a(0)
+    reduce_a(1)
+    reduce_b(0)
+    reduce_a(2)
+    reduce_b(1)
+    reduce_c(0)
+    reduce_a(3)
+    reduce_b(2)
+    reduce_c(1)
+    reduce_d(0)
+    reduce_b(3)
+    reduce_c(2)
+    reduce_d(1)
+    combine(0)
+    reduce_c(3)
+    reduce_d(2)
+    combine(1)
+    reduce_d(3)
+    combine(2)
+    combine(3)
+
+    last = remote(contrib_sib, contrib, pre_s.at[3], pre_r.at[3], sib)
+    last.start()
+    last.wait_recv()
+    cols = pl.ds(pl.multiple_of((1 - core) * half, 128), half)
+    out_ref[:, cols] = (f32(att_ref[:, cols]) + contrib[...]).astype(jnp.bfloat16)
+
+    started = [send_meta, send_nrm, send_down, last] + sent_hidden
+    for c in range(NC):
+        started += dispatches[c] + gather[c] + shares[c] + reduce[c] + returns[c]
+    for copy in started:
+        copy.wait_send()
+
+
+def experts(attended, norm_gain, expert_ids, expert_weights, gate_weight, up_weight, down_weight):
+    d = attended.shape[1]
+    half = d // 2
+    width = half // NC
+    bf, f32 = jnp.bfloat16, jnp.float32
+    meta = jnp.pad(
+        jnp.concatenate([expert_ids.T.astype(f32), expert_weights.T], axis=0), ((0, 4), (0, 112))
+    )
+    vmem = pl.BlockSpec(memory_space=pltpu.VMEM)
+    anyspace = pl.BlockSpec(memory_space=pl.ANY)
+    dma = pltpu.SemaphoreType.DMA
+    block = (8, 16, width)
+    return pl.pallas_call(
+        experts_kernel,
+        out_shape=jax.ShapeDtypeStruct(attended.shape, bf),
+        in_specs=[vmem, vmem, vmem, anyspace, anyspace, anyspace],
+        out_specs=vmem,
+        scratch_shapes=[
+            pltpu.VMEM((d, 768), bf),
+            pltpu.VMEM((768, half), bf),
+            pltpu.VMEM((8, 128), f32),
+            pltpu.VMEM((2, 16, half), bf),
+            pltpu.VMEM((16, half), bf),
+            pltpu.VMEM((NC,) + block, bf),
+            pltpu.VMEM((NC, 8) + block, bf),
+            pltpu.VMEM((NC, 8) + block, bf),
+            pltpu.VMEM((4, 256, 768), f32),
+            pltpu.VMEM((4, 256, 768), bf),
+            pltpu.VMEM((NC, 8) + block, bf),
+            pltpu.VMEM((NC, 2) + block, bf),
+            pltpu.VMEM((NC,) + block, bf),
+            pltpu.VMEM((NC,) + block, bf),
+            pltpu.VMEM((NC, 2, 4, 16, width), bf),
+            pltpu.VMEM((NC, 2) + block, bf),
+            pltpu.VMEM((NC,) + block, bf),
+            pltpu.VMEM((NC,) + block, bf),
+            pltpu.VMEM((16, half), f32),
+            pltpu.VMEM((16, half), f32),
+            dma((3,)),
+            dma((4,)),
+            dma((4,)),
+            dma((NC, 7)),
+            dma((NC, 7)),
+            dma((NC, 8)),
+            dma((NC, 8)),
+            dma((NC, 8)),
+            dma((NC, 8)),
+            dma((4,)),
+            dma((4,)),
+            dma((NC, 8)),
+            dma((NC, 8)),
+            dma((NC, 7)),
+            dma((NC, 7)),
+        ],
+        compiler_params=pltpu.CompilerParams(
+            collective_id=1, has_side_effects=True, vmem_limit_bytes=VMEM_LIMIT
+        ),
+        cost_estimate=pl.CostEstimate(
+            flops=2 * 3 * 1024 * d * 384, bytes_accessed=3 * d * 384 * 2, transcendentals=1024 * 384
+        ),
+        name="experts",
+    )(attended, norm_gain.reshape(1, d), meta, gate_weight, up_weight, down_weight)
 
 
 def row_positions(block_order, start, count, half):
@@ -14,13 +414,6 @@
     )
     first = jnp.sum(table * block_order[None, :], axis=1)
     return first * half + rows % half
-
-
-def slot_table(ids, experts):
-    flat = ids.reshape(-1)
-    onehot = (flat[:, None] == jnp.arange(experts, dtype=jnp.int32)[None, :]).astype(jnp.int32)
-    earlier_mask = jnp.cumsum(onehot, axis=0) - onehot
-    return (flat, jnp.sum(earlier_mask * onehot, axis=1))
 
 
 def on_device(
@@ -84,54 +477,10 @@
         partial_proj.astype(jnp.bfloat16), "exp", scatter_dimension=0, tiled=True
     ).astype(jnp.float32)
     attended = (stream.astype(jnp.float32) + summed_output).astype(jnp.bfloat16)
-    widened = attended.astype(jnp.float32)
-    normed = (
-        widened * lax.rsqrt(jnp.mean(widened * widened, axis=-1, keepdims=True) + 1e-05) * norm_gain
-    ).astype(jnp.bfloat16)
-    capacity = max(2, 4 * moe_rows // n_exp)
-    slots_all = n_exp * capacity
-    slot_range = jnp.arange(slots_all, dtype=jnp.int32)
-    flat, slot = slot_table(expert_ids, n_exp)
-    own_target = (flat * capacity + slot).reshape(moe_rows, 2)
-    match = jnp.any(own_target[:, :, None] == slot_range[None, None, :], axis=1)
-    send = jnp.dot(match.T.astype(jnp.bfloat16), normed, preferred_element_type=jnp.float32).astype(
-        jnp.bfloat16
-    )
-    received = lax.all_to_all(
-        send.reshape(n_exp, capacity, send.shape[1]), "exp", split_axis=0, concat_axis=0, tiled=True
-    )
-    slot_rows = received.reshape(slots_all, send.shape[1])
-    gate_local = gate_weight[0]
-    up_local = up_weight[0]
-    down_local = down_weight[0]
-    piece = lax.all_gather(slot_rows, "ctx", axis=0, tiled=True)
-    gate_part = jnp.dot(piece, gate_local, preferred_element_type=jnp.float32)
-    up_part = jnp.dot(piece, up_local, preferred_element_type=jnp.float32)
-    hidden = (jax.nn.silu(gate_part) * up_part).astype(jnp.bfloat16)
-    expert_out = lax.psum_scatter(
-        jnp.dot(hidden, down_local, preferred_element_type=jnp.float32).astype(jnp.bfloat16),
-        "ctx",
-        scatter_dimension=0,
-        tiled=True,
-    )
-    back = lax.all_to_all(
-        expert_out.reshape(n_exp, capacity, expert_out.shape[1]),
-        "exp",
-        split_axis=0,
-        concat_axis=0,
-        tiled=True,
-    )
-    back = back.reshape(slots_all, expert_out.shape[1])
-    combine = jnp.sum(
-        jnp.where(
-            own_target[:, :, None] == slot_range[None, None, :], expert_weights[:, :, None], 0.0
-        ),
-        axis=1,
-    )
-    mixed_wide = widened + jnp.dot(
-        combine, back.astype(jnp.float32), precision=lax.Precision.HIGHEST
-    )
-    return (attended, mixed_wide.astype(jnp.bfloat16))
+    mixed = experts(
+        attended, norm_gain, expert_ids, expert_weights, gate_weight, up_weight, down_weight
+    )
+    return (attended, mixed)
 
 
 def solution(mesh):

time: 443 us -> 297 us (0.67)
  waiting for transfers between devices: 308 us -> 83.2 us
  Pallas kernels: 0 us -> 126 us
  matrix products: 42.4 us -> 11.2 us
  blocking collectives: 66 us -> 53 us
    pallas_call x0 -> x1, Pallas kernels: none -> 126 us  [experts(): pl.pallas_call(experts_kernel, out_shape=jax.ShapeDtypeStruct(attended.sh...]
    reduce_scatter x1 -> x0, waiting for transfers between devices: 119 us -> none  [on_device(): lax.psum_scatter(jnp.dot(hidden, down_local, preferred_element_type=jnp.f...]
    all_gather x1 -> x0, waiting for transfers between devices: 94.5 us -> none  [on_device(): piece = lax.all_gather(slot_rows, 'ctx', axis=0, tiled=True)]
    dot_general x5 -> x0, matrix products: 31.1 us -> none  [the longest x1 11.1 us: on_device(): gate_part = jnp.dot(piece, gate_local, preferred_element_type=jnp.float32)]
    all_to_all x1 -> x0, blocking collectives: 13.2 us -> none  [on_device(): lax.all_to_all(send.reshape(n_exp, capacity, send.shape[1]), 'exp', split...]
    all_to_all x1 -> x0, waiting for transfers between devices: 11.3 us -> none  [on_device(): lax.all_to_all(expert_out.reshape(n_exp, capacity, expert_out.shape[1]),...]
  transfers between devices with their start and end apart: 5 -> 2, of which waited for: 5 -> 2; matrix products, arithmetic and copies ran while one was open for 2% -> 3% of each run, Pallas kernels for 0% -> 0%
where the time goes in v1:
time: 297 us
  Pallas kernels  126 us (42%)
  waiting for transfers between devices  83.2 us (28%)
  blocking collectives  53 us (18%)
  between operations  14.2 us (5%)
  matrix products  11.2 us (4%)
  other arithmetic  6.15 us (2%)
    pallas_call x1, Pallas kernels, experts(): pl.pallas_call(experts_kernel, out_shape=jax.ShapeDtypeStruct(attended.sh...  126 us
    all_gather x1, waiting for transfers between devices, on_device(): lax.all_gather(out_weight, 'ctx', axis=1, tiled=True)  45.3 us
    reduce_scatter x1, waiting for transfers between devices, on_device(): lax.psum_scatter(partial_proj.astype(jnp.bfloat16), 'exp', scatter_dimens...  37.2 us
    all_gather x1, blocking collectives, on_device(): key_piece = lax.all_gather(key_head_rows, 'ctx', axis=0, tiled=True)  31.1 us
    all_gather x1, blocking collectives, on_device(): value_piece = lax.all_gather(value_head_rows, 'ctx', axis=0, tiled=True)  21.9 us
    dot_general x1, matrix products, on_device(): jnp.dot(heads_out, lax.all_gather(out_weight, 'ctx', axis=1, tiled=True),...  7.68 us
  transfers between devices with their start and end apart: 2, of which 2 were waited for; matrix products, arithmetic and copies ran while one was open for 3% of the time, Pallas kernels for 0%

profile of v1, /device:TPU:1, one launch (start us, length us, event | category | flops | bytes accessed | tf_op | source)
XLA Modules:
  0.0 296.7 jit_solution(9186986419771283129)
XLA Ops:
  7.2 0.0 copy-start
  7.2 0.0 all-gather.2.cloned.1.call-start
  7.2 0.7 all-gather.2.cloned.1.call-update
  7.9 0.0 reduce-scatter.2.cloned.1.call-start
  8.0 0.9 copy.18
  8.9 0.7 select_reduce_fusion.1
  9.6 0.8 select_reduce_fusion
  10.4 31.1 %all_gather.9 = bf16[2048,128]{1,0:T(8,128)(2,1)S(1)} all-gather(bf16[128,128]{1,0:T(8,128)(2,1)} %param.14), channel_id=1, replica_groups=mesh['ctx'=16,'exp'=8] {'ctx'}, dimensions={0}, use_global_device_ids=true | all-gather | bytes 557056 | tf_op jit(solution)/shard_map/all_gather | solution.py:442
  41.5 0.3 broadcast_compare_fusion
  41.9 0.0 copy-done
  41.9 1.4 fusion
  43.2 21.9 %all_gather.10 = bf16[2048,128]{0,1:T(8,128)(2,1)S(1)} all-gather(bf16[128,128]{0,1:T(8,128)(2,1)S(1)} %copy.18), channel_id=1, replica_groups=mesh['ctx'=16,'exp'=8] {'ctx'}, dimensions={0}, use_global_device_ids=true | all-gather | bytes 557056 | tf_op jit(solution)/shard_map/all_gather | solution.py:443
  65.2 2.0 fusion.1
  67.2 2.2 fusion.10
  69.4 45.3 %all-gather.2.cloned.1.call-done = bf16[1024,6144]{1,0:T(8,128)(2,1)} async-done(((bf16[1024,384]{1,0:T(8,128)(2,1)}), bf16[1024,6144]{1,0:T(8,128)(2,1)}) %all-gather.2.cloned.1.call-update) | async-done | bytes 12582928 | tf_op jit(solution)/shard_map/all_gather | solution.py:472
  114.7 0.0 copy-start.2
  114.7 0.0 copy-start.3
  114.7 0.0 copy-start.1
  114.7 7.7 %convolution_convert_fusion = bf16[128,6144]{1,0:T(8,128)(2,1)} fusion(bf16[128,1024]{0,1:T(8,128)(2,1)S(1)} %bitcast.54, bf16[1024,6144]{1,0:T(8,128)(2,1)} %all-gather.2.cloned.1.call-done), kind=kOutput, calls=%fused_computation.3 | convolution fusion | flops 1611399168 | bytes 14417920 | tf_op jit(solution)/shard_map/dot_general | solution.py:470
  122.4 0.0 reduce-scatter.2.cloned.1.call-update
  122.4 0.0 copy-done.2
  122.5 0.0 copy-done.3
  122.5 0.6 select_maximum_fusion.meta_ref
  123.1 37.2 %reduce-scatter.2.cloned.1.call-done = bf16[16,6144]{1,0:T(8,128)(2,1)} async-done(((bf16[128,6144]{1,0:T(8,128)(2,1)}), bf16[16,6144]{1,0:T(8,128)(2,1)}) %reduce-scatter.2.cloned.1.call-update) | async-done | bytes 196624 | tf_op jit(solution)/shard_map/reduce_scatter | solution.py:476
  160.3 0.0 copy-done.1
  160.3 1.6 add_convert_fusion.att_ref
  161.9 126.3 %experts.1 = bf16[16,6144]{1,0:T(8,128)(2,1)} custom-call(bf16[16,6144]{1,0:T(8,128)(2,1)} %add_convert_fusion.att_ref, f32[1,6144]{1,0:T(1,128)} %bitcast.56, f32[8,128]{1,0:T(8,128)} %select_maximum_fusion.meta_ref, bf16[1,6144,384]{2,1,0:T(8,128)(2,1)} %gate_ref.1, bf16[1,6144,384]{2,1,0:T(8,128)(2,1)} %up_ref.1, bf16[1,384,6144]{2,1,0:T(8,128)(2,1)} %down_ref.1), custom_call_target="tpu_custom_call" | custom-call | flops 14495514624 | bytes 14155776 | tf_op jit(solution)/shard_map/experts/pallas_call | solution.py:357
  288.2 1.6 copy.29
  (6 shorter events, 0.0 us)
Async XLA Ops:
  7.2 34.7 %copy-start = (bf16[128,1024]{1,0:T(8,128)(2,1)S(1)}, bf16[128,1024]{1,0:T(8,128)(2,1)}, u32[]{:S(2)}) copy-start(bf16[128,1024]{1,0:T(8,128)(2,1)} %param.13) | copy-start | bytes 786436
  7.2 107.5 %all-gather.2.cloned.1.call-start = ((), (), s32[]{:S(2)}) async-start(), calls=%async_computation.1 | async-start | bytes 13369344 | tf_op jit(solution)/shard_map/all_gather | solution.py:472
  7.9 152.4 %reduce-scatter.2.cloned.1.call-start = ((), (), s32[]{:S(2)}) async-start(), calls=%async_computation.2 | async-start | bytes 1769472 | tf_op jit(solution)/shard_map/reduce_scatter | solution.py:476
  114.7 7.7 %copy-start.2 = (s32[16,2]{0,1:T(2,128)S(1)}, s32[16,2]{0,1:T(2,128)}, u32[]{:S(2)}) copy-start(s32[16,2]{0,1:T(2,128)} %param.22) | copy-start | bytes 388
  114.7 7.7 %copy-start.3 = (f32[16,2]{0,1:T(2,128)S(1)}, f32[16,2]{0,1:T(2,128)}, u32[]{:S(2)}) copy-start(f32[16,2]{0,1:T(2,128)} %param.23) | copy-start | bytes 388
  114.7 45.5 %copy-start.1 = (bf16[16,6144]{1,0:T(8,128)(2,1)S(1)}, bf16[16,6144]{1,0:T(8,128)(2,1)}, u32[]{:S(2)}) copy-start(bf16[16,6144]{1,0:T(8,128)(2,1)} %param.12) | copy-start | bytes 589828
Sparse Core Ops, SparseCore 0:
  10.4 104.3 all-gather.1
  122.6 37.6 reduce-scatter.1

commit v2 on v1

--- a/solution.py
+++ b/solution.py
@@ -406,14 +406,187 @@
     )(attended, norm_gain.reshape(1, d), meta, gate_weight, up_weight, down_weight)
 
 
-def row_positions(block_order, start, count, half):
-    rows = start + jnp.arange(count, dtype=jnp.int32)
-    blocks = rows // half
-    table = (blocks[:, None] == jnp.arange(block_order.shape[0], dtype=jnp.int32)[None, :]).astype(
-        jnp.int32
-    )
-    first = jnp.sum(table * block_order[None, :], axis=1)
-    return first * half + rows % half
+def attention_kernel(
+    q_ref, k_ref, v_ref, qpos_ref, kpos_ref, weight_ref, stream_ref, out_ref,
+    kv, bias, wcat, heads, part, got, summed, blocks,
+    kv_s, kv_r, kvs_s, kvs_r, w_load, w_s, w_r, h_s, h_r, p_s, p_r, c_s, c_r,
+):
+    z, xh, core, exp = place()
+    up_z, down_z, far_z = lax.rem(z + 1, 4), lax.rem(z + 3, 4), lax.rem(z + 2, 4)
+
+    def dev(a, b, c=None, e=None):
+        return (a * 4 + b * 2 + (core if c is None else c), exp if e is None else e)
+
+    def ctx_of(a, b, c):
+        return a * 4 + b * 2 + c
+
+    zp, zm, xp, sib = dev(up_z, xh), dev(down_z, xh), dev(z, 1 - xh), dev(z, xh, 1 - core)
+    turns = [(dz, dx) for dx in (0, 1) for dz in (1, 3, 2, 0) if (dz, dx) != (0, 0)]
+    chips = [(lax.rem(z + dz, 4), lax.rem(xh + dx, 2)) for dz, dx in turns]
+    sources = [(lax.rem(z + 4 - dz, 4), lax.rem(xh + dx, 2)) for dz, dx in turns]
+    peers = [lax.rem(exp + j, 8) for j in range(1, 8)]
+    me = ctx_of(z, xh, core)
+
+    own_cols = pl.ds(pl.multiple_of((xh * 2 + core) * 384, 128), 384)
+    load = pltpu.make_async_copy(weight_ref, wcat.at[:, own_cols], w_load.at[0])
+    load.start()
+    kv[0, me] = k_ref[...]
+    kv[1, me] = v_ref[...]
+    greet([dev(a, b) for a, b in chips] + [sib] + [dev(z, xh, None, e) for e in peers])
+
+    started = []
+
+    def send(src, dst, s, r, device):
+        copy = remote(src, dst, s, r, device)
+        copy.start()
+        started.append(copy)
+        return copy
+
+    gathers = [
+        send(kv.at[:, me], kv.at[:, me], kv_s.at[j], kv_r.at[j], dev(a, b))
+        for j, (a, b) in enumerate(chips)
+    ]
+    shares = [send(kv.at[:, me], kv.at[:, me], kvs_s.at[7], kvs_r.at[7], sib)]
+    w_x = send(weight_ref, wcat.at[:, own_cols], w_s.at[0], w_r.at[0], xp)
+    w_sib = send(weight_ref, wcat.at[:, own_cols], w_s.at[1], w_r.at[1], sib)
+    bias[...] = jnp.where(kpos_ref[...] <= qpos_ref[...], 0.0, -1e30)
+    for j, (a, b) in enumerate(sources):
+        gathers[j].wait_recv()
+        slot = kv.at[:, ctx_of(a, b, core)]
+        shares.append(send(slot, slot, kvs_s.at[j], kvs_r.at[j], sib))
+    for copy in shares:
+        copy.wait_recv()
+
+    scale = PER_LANE_DIM ** (-0.5) * 1.4426950408889634
+
+    def attend(half):
+        def body(i, carry):
+            first = pl.multiple_of(half * 512 + i * 256, 128)
+            pair = q_ref[:, pl.ds(first, 256)]
+            q = jnp.concatenate([pair[:, :128], pair[:, 128:]], axis=0)
+            keys = kv[0].reshape(2048, 128)
+            values = kv[1].reshape(2048, 128)
+            logits = lax.dot_general(
+                q, keys, (((1,), (1,)), ((), ())), preferred_element_type=jnp.float32
+            )
+            logits = logits.reshape(2, 128, 2048) * scale + bias[...][None]
+            peak = jnp.max(logits, axis=-1, keepdims=True)
+            expd = jnp.exp2(logits - peak)
+            total = jnp.sum(expd, axis=-1, keepdims=True)
+            weighted = jnp.dot(
+                expd.astype(jnp.bfloat16).reshape(256, 2048), values, preferred_element_type=jnp.float32
+            )
+            result = (weighted.reshape(2, 128, 128) / total).astype(jnp.bfloat16)
+            out = jnp.concatenate([result[0], result[1]], axis=1)
+            heads[z, half, :, pl.ds(pl.multiple_of(i * 256, 128), 256)] = out
+            return carry
+
+        lax.fori_loop(0, 2, body, 0)
+
+    def send_heads(k, a, half, device):
+        return send(heads.at[a, half], heads.at[a, half], h_s.at[k], h_r.at[k], device)
+
+    attend(0)
+    moves = [send_heads(0, z, 0, zp), send_heads(1, z, 0, zm)]
+    attend(1)
+    moves += [send_heads(2, z, 1, zp), send_heads(3, z, 1, zm)]
+    w_x.wait_recv()
+    other_cols = pl.ds(pl.multiple_of(((1 - xh) * 2 + core) * 384, 128), 384)
+    w_far = send(wcat.at[:, other_cols], wcat.at[:, other_cols], w_s.at[2], w_r.at[2], sib)
+    load.wait()
+    w_sib.wait_recv()
+    w_far.wait_recv()
+
+    def project(t, a):
+        product = jnp.dot(heads[a, 0], wcat[:512, :], preferred_element_type=jnp.float32)
+        product += jnp.dot(heads[a, 1], wcat[512:, :], preferred_element_type=jnp.float32)
+        part[a] = product.astype(jnp.bfloat16).reshape(8, 16, 1536)
+        copies = [
+            send(part.at[a, e], got.at[a, exp], p_s.at[t, j], p_r.at[t, j], dev(z, xh, None, e))
+            for j, e in enumerate(peers)
+        ]
+        got[a, exp] = part[a, exp]
+        return copies
+
+    def add_up(t, a, copies):
+        for copy in copies:
+            copy.wait_recv()
+        total = jnp.sum(got[a].astype(jnp.float32), axis=0).astype(jnp.bfloat16)
+        if t == 0:
+            blocks[z] = total
+            return None
+        summed[a] = total
+        return send(summed.at[a], blocks.at[z], c_s.at[t - 1], c_r.at[t - 1], dev(a, xh))
+
+    sums = [project(0, z)]
+    moves[0].wait_recv()
+    moves.append(send_heads(4, down_z, 0, zp))
+    moves[1].wait_recv()
+    moves[2].wait_recv()
+    moves[3].wait_recv()
+    moves.append(send_heads(5, up_z, 1, zm))
+    sums.append(project(1, down_z))
+    sums.append(project(2, up_z))
+    moves[4].wait_recv()
+    moves[5].wait_recv()
+    sums.append(project(3, far_z))
+    last = [add_up(t, a, sums[t]) for t, a in enumerate((z, down_z, up_z, far_z))]
+    for copy in last[1:]:
+        copy.wait_recv()
+    for a in range(4):
+        cols = slice(a * 1536, (a + 1) * 1536)
+        out_ref[:, cols] = (
+            stream_ref[:, cols].astype(jnp.float32) + blocks[a].astype(jnp.float32)
+        ).astype(jnp.bfloat16)
+    for copy in started:
+        copy.wait_send()
+
+
+def attention(stream, queries, keys, values, block_order, out_weight):
+    bf, f32 = jnp.bfloat16, jnp.float32
+    rows = queries.shape[0]
+    kpos = (block_order[:, None] * 64 + jnp.arange(64, dtype=jnp.int32)[None, :]).reshape(1, 2048)
+    qpos = lax.dynamic_slice_in_dim(kpos, lax.axis_index("ctx") * rows, rows, 1).reshape(rows, 1)
+    vmem = pl.BlockSpec(memory_space=pltpu.VMEM)
+    dma = pltpu.SemaphoreType.DMA
+    return pl.pallas_call(
+        attention_kernel,
+        out_shape=jax.ShapeDtypeStruct(stream.shape, bf),
+        in_specs=[vmem] * 5 + [pl.BlockSpec(memory_space=pl.ANY), vmem],
+        out_specs=vmem,
+        scratch_shapes=[
+            pltpu.VMEM((2, 16, 128, 128), bf),
+            pltpu.VMEM((128, 2048), f32),
+            pltpu.VMEM((1024, 1536), bf),
+            pltpu.VMEM((4, 2, 128, 512), bf),
+            pltpu.VMEM((4, 8, 16, 1536), bf),
+            pltpu.VMEM((4, 8, 16, 1536), bf),
+            pltpu.VMEM((4, 16, 1536), bf),
+            pltpu.VMEM((4, 16, 1536), bf),
+            dma((7,)),
+            dma((7,)),
+            dma((8,)),
+            dma((8,)),
+            dma((1,)),
+            dma((3,)),
+            dma((3,)),
+            dma((6,)),
+            dma((6,)),
+            dma((4, 7)),
+            dma((4, 7)),
+            dma((3,)),
+            dma((3,)),
+        ],
+        compiler_params=pltpu.CompilerParams(
+            collective_id=0, has_side_effects=True, vmem_limit_bytes=VMEM_LIMIT
+        ),
+        cost_estimate=pl.CostEstimate(
+            flops=2 * 1024 * 128 * 2048 * 2 + 2 * 512 * 1024 * 1536,
+            bytes_accessed=1024 * 384 * 2,
+            transcendentals=1024 * 2048,
+        ),
+        name="attention",
+    )(queries, keys, values, qpos, kpos, out_weight, stream)
 
 
 def on_device(
@@ -430,53 +603,7 @@
     expert_ids,
     expert_weights,
 ):
-    n_exp = lax.axis_size("exp")
-    block_rows = queries.shape[0]
-    half = block_rows // 2
-    heads = queries.shape[1] // PER_LANE_DIM
-    kv_heads = key_head_rows.shape[1] // PER_LANE_DIM
-    head_group = heads // kv_heads
-    query_pos = row_positions(block_order, lax.axis_index("ctx") * block_rows, block_rows, half)
-    heads_of_query = queries.reshape(block_rows, kv_heads, head_group, PER_LANE_DIM)
-    running_max = jnp.full((kv_heads, head_group, block_rows), -1e30, jnp.float32)
-    key_piece = lax.all_gather(key_head_rows, "ctx", axis=0, tiled=True)
-    value_piece = lax.all_gather(value_head_rows, "ctx", axis=0, tiled=True)
-    count = key_piece.shape[0]
-    key_pos = row_positions(block_order, jnp.int32(0), count, half)
-    heads_of_key = key_piece.reshape(count, kv_heads, PER_LANE_DIM)
-    heads_of_value = value_piece.reshape(count, kv_heads, PER_LANE_DIM)
-    similarity_logits = jnp.einsum(
-        "rkgd,tkd->kgrt", heads_of_query, heads_of_key, preferred_element_type=jnp.float32
-    ) * PER_LANE_DIM ** (-0.5)
-    visible = key_pos[None, :] <= query_pos[:, None]
-    similarity_logits = jnp.where(visible, similarity_logits, -1e30)
-    new_max = jnp.maximum(running_max, jnp.max(similarity_logits, axis=-1))
-    expd = jnp.where(visible, jnp.exp(similarity_logits - new_max[..., None]), 0.0)
-    total = jnp.sum(expd, axis=-1)
-    product = jnp.einsum(
-        "kgrt,tkd->kgrd",
-        expd.astype(jnp.bfloat16),
-        heads_of_value,
-        preferred_element_type=jnp.float32,
-    )
-    weighted = product
-    running_max, total, weighted = (new_max, total, weighted)
-    heads_out = (
-        (weighted / total[..., None])
-        .transpose(2, 0, 1, 3)
-        .reshape(block_rows, heads * PER_LANE_DIM)
-        .astype(jnp.bfloat16)
-    )
-    partial_proj = jnp.dot(
-        heads_out,
-        lax.all_gather(out_weight, "ctx", axis=1, tiled=True),
-        preferred_element_type=jnp.float32,
-    )
-    moe_rows = stream.shape[0]
-    summed_output = lax.psum_scatter(
-        partial_proj.astype(jnp.bfloat16), "exp", scatter_dimension=0, tiled=True
-    ).astype(jnp.float32)
-    attended = (stream.astype(jnp.float32) + summed_output).astype(jnp.bfloat16)
+    attended = attention(stream, queries, key_head_rows, value_head_rows, block_order, out_weight)
     mixed = experts(
         attended, norm_gain, expert_ids, expert_weights, gate_weight, up_weight, down_weight
     )

time: 297 us -> 189 us (0.64)
  waiting for transfers between devices: 83.2 us -> 0 us
  Pallas kernels: 126 us -> 182 us
  blocking collectives: 53 us -> 0 us
  between operations: 14.2 us -> 0.68 us
  matrix products: 11.2 us -> 0 us
  other arithmetic: 6.15 us -> 2.69 us
    pallas_call x0 -> x1, Pallas kernels: none -> 60.2 us  [attention(): pl.pallas_call(attention_kernel, out_shape=jax.ShapeDtypeStruct(stream.sh...]
    all_gather x2 -> x0, blocking collectives: 53 us -> none  [the longest x1 31.1 us: on_device(): key_piece = lax.all_gather(key_head_rows, 'ctx', axis=0, tiled=True)]
    all_gather x1 -> x0, waiting for transfers between devices: 45.3 us -> none  [on_device(): lax.all_gather(out_weight, 'ctx', axis=1, tiled=True)]
    reduce_scatter x1 -> x0, waiting for transfers between devices: 37.2 us -> none  [on_device(): lax.psum_scatter(partial_proj.astype(jnp.bfloat16), 'exp', scatter_dimens...]
    dot_general x3 -> x0, matrix products: 11.2 us -> none  [the longest x1 7.68 us: on_device(): jnp.dot(heads_out, lax.all_gather(out_weight, 'ctx', axis=1, tiled=True),...]
    pallas_call x1, Pallas kernels: 126 us -> 122 us  [experts(): pl.pallas_call(experts_kernel, out_shape=jax.ShapeDtypeStruct(attended.sh...]
    reduce_sum x3 -> x0, other arithmetic: 3.52 us -> none  [the longest x1 2.01 us: on_device(): total = jnp.sum(expd, axis=-1)]
  transfers between devices with their start and end apart: 2 -> 0, of which waited for: 2 -> 0; matrix products, arithmetic and copies ran while one was open for 3% -> 0% of each run, Pallas kernels for 0% -> 0%
where the time goes in v2:
time: 189 us
  Pallas kernels  182 us (96%)
  local copies, waits for them, and re-layouts  3.14 us (2%)
  other arithmetic  2.69 us (1%)
    pallas_call x1, Pallas kernels, experts(): pl.pallas_call(experts_kernel, out_shape=jax.ShapeDtypeStruct(attended.sh...  122 us
    pallas_call x1, Pallas kernels, attention(): pl.pallas_call(attention_kernel, out_shape=jax.ShapeDtypeStruct(stream.sh...  60.2 us

profile of v2, /device:TPU:1, one launch (start us, length us, event | category | flops | bytes accessed | tf_op | source)
XLA Modules:
  0.0 188.9 jit_solution(5027989850473152168)
XLA Ops:
  0.6 0.7 broadcast_multiply_fusion
  1.3 0.7 convert_bitcast_fusion
  2.0 1.3 select_maximum_fusion.meta_ref
  3.3 0.1 iota_add_fusion
  3.3 0.1 add.31.kpos_ref
  3.4 0.0 copy-start.1
  3.4 0.7 copy.14.qpos_ref
  4.2 0.0 copy-done.1
  4.2 60.2 %attention.1.att_ref = bf16[16,6144]{1,0:T(8,128)(2,1)} custom-call(bf16[128,1024]{1,0:T(8,128)(2,1)} %q_ref.1, bf16[128,128]{1,0:T(8,128)(2,1)} %k_ref.1, bf16[128,128]{1,0:T(8,128)(2,1)} %v_ref.1, s32[128,1]{1,0:T(8,128)} %copy.14.qpos_ref, s32[1,2048]{1,0:T(1,128)} %copy-done.1, bf16[1024,384]{1,0:T(8,128)(2,1)} %weight_ref.1, bf16[16,6144]{1,0:T(8,128)(2,1)} %stream_ref.1), custom_call_target="tpu_custom_call" | custom-call | flops 2684354560 | bytes 786432 | tf_op jit(solution)/shard_map/attention/pallas_call | solution.py:552
  64.3 0.0 copy-start
  64.4 122.2 %experts.1 = bf16[16,6144]{1,0:T(8,128)(2,1)} custom-call(bf16[16,6144]{1,0:T(8,128)(2,1)} %attention.1.att_ref, f32[1,6144]{1,0:T(1,128)} %bitcast.7, f32[8,128]{1,0:T(8,128)} %select_maximum_fusion.meta_ref, bf16[1,6144,384]{2,1,0:T(8,128)(2,1)} %gate_ref.1, bf16[1,6144,384]{2,1,0:T(8,128)(2,1)} %up_ref.1, bf16[1,384,6144]{2,1,0:T(8,128)(2,1)} %down_ref.1), custom_call_target="tpu_custom_call" | custom-call | flops 14495514624 | bytes 14155776 | tf_op jit(solution)/shard_map/experts/pallas_call | solution.py:357
  186.6 0.0 copy-done
  186.6 0.7 copy.17
  187.2 1.6 copy.18
  (1 shorter events, 0.0 us)
Async XLA Ops:
  3.4 0.8 copy-start.1
  64.3 122.2 %copy-start = (bf16[16,6144]{1,0:T(8,128)(2,1)S(1)}, bf16[16,6144]{1,0:T(8,128)(2,1)}, u32[]{:S(2)}) copy-start(bf16[16,6144]{1,0:T(8,128)(2,1)} %attention.1.att_ref) | copy-start | bytes 589828

commit v3 on v0

v3 whole, which is shorter than its diff:
```python
import jax
import jax.numpy as jnp
from jax import lax
from jax.experimental import pallas as pl
from jax.experimental.pallas import tpu as pltpu
from jax.sharding import PartitionSpec as P

HEAD = 128
MESH = pl.DeviceIdType.MESH
VMEM_LIMIT = 62 * 2**20
WIDTHS = (384, 768, 768, 768, 384)
NC = len(WIDTHS)
STARTS = tuple(sum(WIDTHS[:c]) for c in range(NC))
BF16, F32 = jnp.bfloat16, jnp.float32


def f32(value):
    return value.astype(F32)


def dot(a, b):
    return jnp.dot(a, b, preferred_element_type=F32)


def remote(src, dst, send, recv, device):
    return pltpu.make_async_remote_copy(
        src_ref=src, dst_ref=dst, send_sem=send, recv_sem=recv, device_id=device, device_id_type=MESH
    )


def greet(devices):
    barrier = pltpu.get_barrier_semaphore()
    for device in devices:
        pl.semaphore_signal(barrier, inc=1, device_id=device, device_id_type=MESH)
    pl.semaphore_wait(barrier, len(devices))


def slot_match(meta, core):
    row = lax.broadcasted_iota(jnp.int32, (128, 128), 0)
    lane = lax.broadcasted_iota(jnp.int32, (128, 128), 1)
    expert = f32(row // 16)
    first = (meta[0:1, :] == expert) & (lane < 16)
    second = (meta[1:2, :] == expert) & (lane < 16)
    named = jnp.where(first | second, 1.0, 0.0)
    earlier = jnp.where(row < lane, 1.0, 0.0)
    rank = dot(named.astype(BF16), earlier.astype(BF16))
    slot = f32(lax.rem(row, 8))
    mine = lax.rem(row // 8, 2) == core
    match = jnp.where((rank == slot) & mine, named, 0.0)
    weight = match * jnp.where(first, meta[2:3, :], meta[3:4, :])
    return match[:, :16].astype(BF16), weight.T[:16, :]


def staged(count, *stages):
    for step in range(count + max(late for late, _ in stages)):
        for late, stage in stages:
            if 0 <= step - late < count:
                stage(step - late)


def layer_kernel(
    q_ref, k_ref, v_ref, order_ref, proj_ref, stream_ref, gain_ref, ids_ref, mix_ref,
    gate_ref, up_ref, down_ref, att_ref, out_ref,
    kv, kpos, bias, wcat, heads, proj, got_y, sums, half_sum, got_x, summed, blocks,
    wgu, wd, meta, meta_sib, nrm, nsib, disp, rows, rows_sib, acc, hid, part,
    got1, got2, got3, got4, got5, final, back, contrib, contrib_sib,
    load_sem, pre_s, pre_r, kv_s, kv_r, w_s, w_r, h_s, h_r, y_s, y_r, x_s, x_r, b_s, b_r,
    disp_s, disp_r, ga_s, ga_r, sib_s, sib_r, hid_s, hid_r, rs_s, rs_r, back_s, back_r,
):
    ctx = lax.axis_index("ctx")
    exp = lax.axis_index("exp")
    z, xh, core = ctx // 4, lax.rem(ctx // 2, 2), lax.rem(ctx, 2)
    y, xl = exp // 2, lax.rem(exp, 2)
    up_z, down_z, far_z = lax.rem(z + 1, 4), lax.rem(z + 3, 4), lax.rem(z + 2, 4)
    half = sum(WIDTHS)

    def dev(a, b, c=None, e=None):
        return (a * 4 + b * 2 + (core if c is None else c), exp if e is None else e)

    def blk(a, b):
        return a * 2 + b

    zp, zm, xp, sib = dev(up_z, xh), dev(down_z, xh), dev(z, 1 - xh), dev(z, xh, 1 - core)
    peers = [lax.rem(exp + j, 8) for j in range(1, 8)]
    columns = [lax.rem(y + j, 4) for j in range(1, 4)]
    own = blk(z, xh)
    far = dev(far_z, xh)
    started = []

    def send(src, dst, s, r, device):
        copy = remote(src, dst, s, r, device)
        copy.start()
        started.append(copy)
        return copy

    def spread(view, s, r):
        copies = [None] * 8

        def forward(k, block, device, piece=None):
            ref = view(block, piece)
            copies[k] = send(ref, ref, s.at[k], r.at[k], device)

        def first():
            forward(0, own, zp)
            forward(1, own, zm)
            forward(2, own, xp)

        def second():
            copies[0].wait_recv()
            forward(3, blk(down_z, xh), zp, 0)
            copies[1].wait_recv()
            forward(4, blk(up_z, xh), zm, 1)
            copies[2].wait_recv()
            forward(5, blk(z, 1 - xh), zp)
            forward(6, blk(z, 1 - xh), zm)

        def third():
            copies[3].wait_recv()
            copies[4].wait_recv()
            forward(7, blk(far_z, xh), xp)

        def fourth():
            copies[5].wait_recv()
            copies[6].wait_recv()
            copies[7].wait_recv()

        return first, second, third, fourth

    def proj_cols(a, b):
        return pl.ds(pl.multiple_of((a * 2 + b) * 384, 128), 384)

    own_cols = proj_cols(xh, core)
    core_cols = pl.ds(pl.multiple_of(core * 384, 128), 384)
    core_half = pl.ds(pl.multiple_of(core * half, 128), half)
    sib_half = pl.ds(pl.multiple_of((1 - core) * half, 128), half)
    loads = [
        pltpu.make_async_copy(proj_ref, wcat.at[:, own_cols], load_sem.at[0]),
        pltpu.make_async_copy(gate_ref.at[0], wgu.at[:, pl.ds(0, 384)], load_sem.at[1]),
        pltpu.make_async_copy(up_ref.at[0], wgu.at[:, pl.ds(384, 384)], load_sem.at[2]),
        pltpu.make_async_copy(down_ref.at[0, :, core_half], wd.at[core_cols], load_sem.at[3]),
    ]
    for load in loads:
        load.start()
    kv[core, xh, z, 0] = k_ref[...]
    kv[core, xh, z, 1] = v_ref[...]
    meta[...] = jnp.zeros_like(meta)
    meta[0:2, 0:16] = f32(ids_ref[...])
    meta[2:4, 0:16] = mix_ref[...]
    greet([zp, zm, far, xp, sib] + [dev(z, xh, None, e) for e in peers])

    def send_kv(k, a, b, device):
        return send(kv.at[core, a, b], kv.at[core, a, b], kv_s.at[k], kv_r.at[k], device)

    from_x = send_kv(0, xh, z, xp)
    column = [send_kv(1 + j, xh, z, device) for j, device in enumerate((zp, zm, far))]
    piece = 256
    send_w = [
        send(
            proj_ref.at[pl.ds(i * piece, piece)], wcat.at[pl.ds(i * piece, piece), own_cols],
            w_s.at[i], w_r.at[i], xp,
        )
        for i in range(4)
    ]
    send_w_sib = send(proj_ref, wcat.at[:, own_cols], pre_s.at[0], pre_r.at[0], sib)
    send_meta = send(meta, meta_sib, pre_s.at[1], pre_r.at[1], sib)
    from_x.wait_recv()
    column += [send_kv(4 + j, 1 - xh, z, device) for j, device in enumerate((zp, zm, far))]
    lane = lax.broadcasted_iota(jnp.int32, (1, 128), 1)
    for slot in range(16):
        place = slot % 4 * 4 + slot // 4 % 2 * 2 + slot // 8
        first = jnp.where(lane < 64, order_ref[2 * place], order_ref[2 * place + 1])
        kpos[:, slot * 128 : (slot + 1) * 128] = first * 64 + lax.rem(lane, 64)
    row = lax.broadcasted_iota(jnp.int32, (128, 1), 0)
    qpos = jnp.where(row < 64, order_ref[2 * ctx], order_ref[2 * ctx + 1]) * 64 + lax.rem(row, 64)
    bias[...] = jnp.where(kpos[...] <= qpos, 0.0, -1e30)
    match_own, weight_own = slot_match(meta[...], core)
    for copy in column[:3]:
        copy.wait_recv()
    share_kv = [send(kv.at[core, xh], kv.at[core, xh], kv_s.at[7], kv_r.at[7], sib)]
    send_meta.wait_recv()
    match_sib, weight_sib = slot_match(meta_sib[...], 1 - core)
    for copy in column[3:]:
        copy.wait_recv()
    share_kv.append(send(kv.at[core, 1 - xh], kv.at[core, 1 - xh], kv_s.at[8], kv_r.at[8], sib))
    for copy in share_kv:
        copy.wait_recv()

    scale = HEAD ** (-0.5) * 1.4426950408889634

    def attend(part_of):
        def body(i, carry):
            pair = q_ref[:, pl.ds(pl.multiple_of(part_of * 512 + i * 256, 128), 256)]
            q = jnp.concatenate([pair[:, :128], pair[:, 128:]], axis=0)
            keys = kv[:, :, :, 0].reshape(2048, HEAD)
            values = kv[:, :, :, 1].reshape(2048, HEAD)
            logits = lax.dot_general(q, keys, (((1,), (1,)), ((), ())), preferred_element_type=F32)
            logits = logits.reshape(2, 128, 2048) * scale + bias[...][None]
            expd = jnp.exp2(logits - jnp.max(logits, axis=-1, keepdims=True))
            total = jnp.sum(expd, axis=-1, keepdims=True)
            weighted = dot(expd.astype(BF16).reshape(256, 2048), values)
            result = (weighted.reshape(2, 128, HEAD) / total).astype(BF16)
            heads[part_of, z, :, pl.ds(pl.multiple_of(i * 256, 128), 256)] = jnp.concatenate(
                [result[0], result[1]], axis=1
            )
            return carry

        lax.fori_loop(0, 2, body, 0)

    def send_heads(i, k, a, rows_of, device):
        view = heads.at[i, a, rows_of]
        return send(view, view, h_s.at[i, k], h_r.at[i, k], device)

    moves = []
    for i in range(2):
        attend(i)
        moves.append([send_heads(i, k, z, pl.ds(0, 128), device) for k, device in enumerate((zp, zm))])
    send_down = send(down_ref.at[0, :, sib_half], wd.at[core_cols], pre_s.at[2], pre_r.at[2], sib)
    far_w = []
    for i in range(4):
        send_w[i].wait_recv()
        view = wcat.at[pl.ds(i * piece, piece), proj_cols(1 - xh, core)]
        far_w.append(send(view, view, w_s.at[4 + i], w_r.at[4 + i], sib))
    for i in range(2):
        moves[i][0].wait_recv()
        moves[i].append(send_heads(i, 2, down_z, pl.ds(0, 64), zp))
        moves[i][1].wait_recv()
        moves[i].append(send_heads(i, 3, up_z, pl.ds(64, 64), zm))
    loads[0].wait()
    send_w_sib.wait_recv()
    for copy in far_w:
        copy.wait_recv()

    order = [z, down_z, up_z, far_z]
    to_y = [None] * 4
    to_x = [None] * 4
    to_block = [None] * 4

    def project(*turns):
        places = [order[t] for t in turns]
        product = 0.0
        for i in range(2):
            lhs = jnp.concatenate([heads[i, b] for b in places], axis=0)
            product += dot(lhs, wcat[i * 512 : (i + 1) * 512, :])
        for n, (t, b) in enumerate(zip(turns, places)):
            proj[b] = product[n * 128 : (n + 1) * 128].astype(BF16).reshape(4, 2, 16, 1536)
            to_y[t] = [
                send(proj.at[b, c], got_y.at[b, y], y_s.at[t, j], y_r.at[t, j], dev(z, xh, None, c * 2 + xl))
                for j, c in enumerate(columns)
            ]
            got_y[b, y] = proj[b, y]

    def add_y(*turns):
        for t in turns:
            b = order[t]
            for copy in to_y[t]:
                copy.wait_recv()
            sums[b] = jnp.sum(f32(got_y[b]), axis=0)
            half_sum[b] = sums[b, 1 - xl].astype(BF16)
            to_x[t] = send(
                half_sum.at[b], got_x.at[b], x_s.at[t], x_r.at[t], dev(z, xh, None, y * 2 + 1 - xl)
            )

    def add_x(*turns):
        for t in turns:
            b = order[t]
            to_x[t].wait_recv()
            total = (sums[b, xl] + f32(got_x[b])).astype(BF16)
            if t == 0:
                blocks[z] = total
            else:
                summed[b] = total
                to_block[t] = send(
                    summed.at[b], blocks.at[z], b_s.at[t - 1], b_r.at[t - 1], dev(b, xh)
                )

    project(0)
    project(1, 2)
    add_y(0)
    for i in range(2):
        moves[i][2].wait_recv()
        moves[i][3].wait_recv()
    project(3)
    add_x(0)
    add_y(1, 2)
    add_x(1, 2)
    add_y(3)
    add_x(3)
    for copy in to_block[1:]:
        copy.wait_recv()
    square = jnp.zeros((16, 1), F32)
    for b in range(4):
        cols = slice(b * 1536, (b + 1) * 1536)
        attended = (f32(stream_ref[:, cols]) + f32(blocks[b])).astype(BF16)
        att_ref[:, cols] = attended
        square += jnp.sum(f32(attended) * f32(attended), axis=-1, keepdims=True)
    normed = f32(att_ref[...]) * lax.rsqrt(square / (2 * half) + 1e-05) * gain_ref[...]
    nrm[0] = normed[:, :half].astype(BF16)
    nrm[1] = normed[:, half:].astype(BF16)
    send_nrm = send(nrm.at[1 - core], nsib, pre_s.at[3], pre_r.at[3], sib)
    send_nrm.wait_recv()

    dispatches = [None] * NC
    shares = [[] for _ in range(NC)]

    def dispatch(c):
        cols = pl.ds(STARTS[c], WIDTHS[c])
        picked = dot(match_own, nrm[core, :, cols]) + dot(match_sib, nsib[:, cols])
        disp[c][...] = picked.astype(BF16).reshape(8, 16, WIDTHS[c])
        dispatches[c] = [
            send(disp[c].at[e], rows[c].at[own, exp], disp_s.at[c, j], disp_r.at[c, j], dev(z, xh, None, e))
            for j, e in enumerate(peers)
        ]
        rows[c][own, exp] = disp[c][exp]

    def row_view(c):
        def view(block, piece):
            if piece is None:
                return rows[c].at[block]
            return rows[c].at[block, pl.ds(piece * 4, 4)]

        return view

    gather = [spread(row_view(c), ga_s.at[c], ga_r.at[c]) for c in range(NC)]

    def share(c, a):
        j = len(shares[c])
        pair = pl.ds(a * 2, 2)
        shares[c].append(send(rows[c].at[pair], rows_sib[c].at[pair], sib_s.at[c, j], sib_r.at[c, j], sib))

    def gather_a(c):
        for copy in dispatches[c]:
            copy.wait_recv()
        gather[c][0]()

    def gather_b(c):
        gather[c][1]()
        share(c, z)

    def gather_c(c):
        gather[c][2]()

    def gather_d(c):
        gather[c][3]()
        share(c, down_z)
        share(c, up_z)
        share(c, far_z)

    def term(source, c, base, i):
        lhs = source[c][pl.ds(i * 2, 2)].reshape(256, WIDTHS[c])
        return dot(lhs, wgu[pl.ds(pl.multiple_of(base + STARTS[c], 128), WIDTHS[c]), :])

    def multiply_own(c):
        if c == 0:
            loads[1].wait()
            loads[2].wait()

        def body(i, carry):
            value = term(rows, c, core * half, i)
            acc[i] = value if c == 0 else acc[i] + value
            return carry

        lax.fori_loop(0, 4, body, 0)

    sent_hidden = []

    def multiply_sib(c):
        for copy in shares[c]:
            copy.wait_recv()

        def body(i, carry):
            acc[i] += term(rows_sib, c, (1 - core) * half, i)
            return carry

        if c < NC - 1:
            lax.fori_loop(0, 4, body, 0)
            return
        for i in range(4):
            value = acc[i] + term(rows_sib, c, (1 - core) * half, i)
            gate_part, up_part = value[:, :384], value[:, 384:]
            hid[i, :, core_cols] = (gate_part / (1.0 + jnp.exp(-gate_part)) * up_part).astype(BF16)
            view = hid.at[i, :, core_cols]
            sent_hidden.append(send(view, view, hid_s.at[i], hid_r.at[i], sib))

    dispatch(0)
    dispatch(1)
    staged(
        NC,
        (0, gather_a),
        (-2, dispatch),
        (1, gather_b),
        (2, gather_c),
        (3, gather_d),
        (3, multiply_own),
        (4, multiply_sib),
    )
    loads[3].wait()
    send_down.wait_recv()

    reduce = [[None] * 8 for _ in range(NC)]
    returns = [None] * NC

    def send_sum(c, k, src, dst, device):
        reduce[c][k] = send(src, dst, rs_s.at[c, k], rs_r.at[c, k], device)

    def reduce_a(c):
        def body(i, carry):
            out = dot(hid[i], wd[:, STARTS[c] : STARTS[c] + WIDTHS[c]])
            part[c][pl.ds(i * 2, 2)] = out.astype(BF16).reshape(2, 8, 16, WIDTHS[c])
            return carry

        if c == 0:
            for i in range(4):
                sent_hidden[i].wait_recv()
                body(i, 0)
        else:
            lax.fori_loop(0, 4, body, 0)
        send_sum(c, 0, part[c].at[blk(up_z, 1 - xh)], got1[c].at[0], zp)
        send_sum(c, 1, part[c].at[blk(down_z, 1 - xh)], got1[c].at[1], zm)
        send_sum(c, 2, part[c].at[blk(far_z, 1 - xh)], got2[c], xp)

    def reduce_b(c):
        reduce[c][2].wait_recv()
        block = blk(far_z, xh)
        part[c][block] = (f32(part[c][block]) + f32(got2[c][...])).astype(BF16)
        send_sum(c, 3, part[c].at[block, pl.ds(0, 4)], got4[c].at[0], zm)
        send_sum(c, 4, part[c].at[block, pl.ds(4, 4)], got4[c].at[1], zp)
        reduce[c][0].wait_recv()
        reduce[c][1].wait_recv()
        block = blk(z, 1 - xh)
        part[c][block] = (f32(part[c][block]) + f32(got1[c][0]) + f32(got1[c][1])).astype(BF16)
        send_sum(c, 5, part[c].at[block], got3[c], xp)

    def reduce_c(c):
        reduce[c][3].wait_recv()
        block = blk(down_z, xh)
        part[c][block, 0:4] = (f32(part[c][block, 0:4]) + f32(got4[c][0])).astype(BF16)
        send_sum(c, 6, part[c].at[block], got5[c].at[0], zm)
        reduce[c][4].wait_recv()
        block = blk(up_z, xh)
        part[c][block, 4:8] = (f32(part[c][block, 4:8]) + f32(got4[c][1])).astype(BF16)
        send_sum(c, 7, part[c].at[block], got5[c].at[1], zp)

    def reduce_d(c):
        for k in (5, 6, 7):
            reduce[c][k].wait_recv()
        final[c][...] = (f32(part[c][own]) + f32(got3[c][...]) + (f32(got5[c][0]) + f32(got5[c][1]))).astype(BF16)
        returns[c] = [
            send(final[c].at[e], back[c].at[exp], back_s.at[c, j], back_r.at[c, j], dev(z, xh, None, e))
            for j, e in enumerate(peers)
        ]
        back[c][exp] = final[c][exp]

    def weigh(weight, values):
        return jnp.dot(weight, values, precision=lax.Precision.HIGHEST, preferred_element_type=F32)

    def combine(c):
        for copy in returns[c]:
            copy.wait_recv()
        values = f32(back[c][...].reshape(128, WIDTHS[c]))
        contrib_sib[:, STARTS[c] : STARTS[c] + WIDTHS[c]] = weigh(weight_sib, values)
        cols = pl.ds(pl.multiple_of(core * half + STARTS[c], 128), WIDTHS[c])
        out_ref[:, cols] = (f32(att_ref[:, cols]) + weigh(weight_own, values)).astype(BF16)

    staged(NC, (0, reduce_a), (1, reduce_b), (2, reduce_c), (3, reduce_d), (4, combine))

    last = send(contrib_sib, contrib, pre_s.at[4], pre_r.at[4], sib)
    last.wait_recv()
    out_ref[:, sib_half] = (f32(att_ref[:, sib_half]) + contrib[...]).astype(BF16)
    for copy in started:
        copy.wait_send()


def on_device(
    stream,
    queries,
    key_head_rows,
    value_head_rows,
    block_order,
    out_weight,
    norm_gain,
    gate_weight,
    up_weight,
    down_weight,
    expert_ids,
    expert_weights,
):
    d = stream.shape[1]
    half = d // 2
    vmem = pl.BlockSpec(memory_space=pltpu.VMEM)
    smem = pl.BlockSpec(memory_space=pltpu.SMEM)
    anyspace = pl.BlockSpec(memory_space=pl.ANY)

    def per_chunk(*shape):
        return [pltpu.VMEM(shape + (width,), BF16) for width in WIDTHS]

    def sems(*shapes):
        return [pltpu.SemaphoreType.DMA(shape) for shape in shapes for _ in range(2)]

    return pl.pallas_call(
        layer_kernel,
        out_shape=(jax.ShapeDtypeStruct(stream.shape, BF16),) * 2,
        in_specs=[vmem, vmem, vmem, smem, anyspace, vmem, vmem, vmem, vmem, anyspace, anyspace, anyspace],
        out_specs=(vmem, vmem),
        scratch_shapes=[
            pltpu.VMEM((2, 2, 4, 2, 128, 128), BF16),
            pltpu.VMEM((1, 2048), jnp.int32),
            pltpu.VMEM((128, 2048), F32),
            pltpu.VMEM((1024, 1536), BF16),
            pltpu.VMEM((2, 4, 128, 512), BF16),
            pltpu.VMEM((4, 4, 2, 16, 1536), BF16),
            pltpu.VMEM((4, 4, 2, 16, 1536), BF16),
            pltpu.VMEM((4, 2, 16, 1536), F32),
            pltpu.VMEM((4, 16, 1536), BF16),
            pltpu.VMEM((4, 16, 1536), BF16),
            pltpu.VMEM((4, 16, 1536), BF16),
            pltpu.VMEM((4, 16, 1536), BF16),
            pltpu.VMEM((d, 768), BF16),
            pltpu.VMEM((768, half), BF16),
            pltpu.VMEM((8, 128), F32),
            pltpu.VMEM((8, 128), F32),
            pltpu.VMEM((2, 16, half), BF16),
            pltpu.VMEM((16, half), BF16),
            per_chunk(8, 16),
            per_chunk(8, 8, 16),
            per_chunk(8, 8, 16),
            pltpu.VMEM((4, 256, 768), F32),
            pltpu.VMEM((4, 256, 768), BF16),
            per_chunk(8, 8, 16),
            per_chunk(2, 8, 16),
            per_chunk(8, 16),
            per_chunk(8, 16),
            per_chunk(2, 4, 16),
            per_chunk(2, 8, 16),
            per_chunk(8, 16),
            per_chunk(8, 16),
            pltpu.VMEM((16, half), F32),
            pltpu.VMEM((16, half), F32),
            pltpu.SemaphoreType.DMA((4,)),
        ]
        + sems(
            (5,), (9,), (8,), (2, 4), (4, 3), (4,), (3,),
            (NC, 7), (NC, 8), (NC, 4), (4,), (NC, 8), (NC, 7),
        ),
        compiler_params=pltpu.CompilerParams(
            collective_id=0, has_side_effects=True, vmem_limit_bytes=VMEM_LIMIT
        ),
        cost_estimate=pl.CostEstimate(
            flops=2 * 3 * 1024 * d * 384 + 4 * 1024 * 128 * 2048 + 2 * 1024 * 1024 * 768,
            bytes_accessed=3 * d * 384 * 2,
            transcendentals=1024 * 2048 + 1024 * 384,
        ),
        name="layer",
    )(
        queries, key_head_rows, value_head_rows, block_order, out_weight, stream, norm_gain.reshape(1, d),
        expert_ids.T, expert_weights.T, gate_weight, up_weight, down_weight,
    )


def solution(mesh):
    in_specs = (
        P(("ctx", "exp"), None),
        P("ctx", "exp"),
        P("ctx", "exp"),
        P("ctx", "exp"),
        P(),
        P("exp", "ctx"),
        P(),
        P("exp", None, "ctx"),
        P("exp", None, "ctx"),
        P("exp", "ctx", None),
        P(("ctx", "exp"), None),
        P(("ctx", "exp"), None),
    )
    out_specs = (P(("ctx", "exp"), None), P(("ctx", "exp"), None))
    return jax.shard_map(
        on_device, mesh=mesh, in_specs=in_specs, out_specs=out_specs, check_vma=False
    )
```

time: 443 us -> 177 us (0.40)
  waiting for transfers between devices: 308 us -> 0 us
  Pallas kernels: 0 us -> 173 us
  blocking collectives: 66 us -> 0 us
  matrix products: 42.4 us -> 0 us
  between operations: 14 us -> 0.64 us
  other arithmetic: 5.48 us -> 0 us
    pallas_call x0 -> x1, Pallas kernels: none -> 173 us  [on_device(): pl.pallas_call(layer_kernel, out_shape=(jax.ShapeDtypeStruct(stream.shape...]
    reduce_scatter x2 -> x0, waiting for transfers between devices: 156 us -> none  [the longest x1 119 us: on_device(): lax.psum_scatter(jnp.dot(hidden, down_local, preferred_element_type=jnp.f...]
    all_gather x2 -> x0, waiting for transfers between devices: 140 us -> none  [the longest x1 94.5 us: on_device(): piece = lax.all_gather(slot_rows, 'ctx', axis=0, tiled=True)]
    all_gather x2 -> x0, blocking collectives: 52.8 us -> none  [the longest x1 31.1 us: on_device(): key_piece = lax.all_gather(key_head_rows, 'ctx', axis=0, tiled=True)]
    dot_general x8 -> x0, matrix products: 42.4 us -> none  [the longest x1 11.1 us: on_device(): gate_part = jnp.dot(piece, gate_local, preferred_element_type=jnp.float32)]
    all_to_all x1 -> x0, blocking collectives: 13.2 us -> none  [on_device(): lax.all_to_all(send.reshape(n_exp, capacity, send.shape[1]), 'exp', split...]
    all_to_all x1 -> x0, waiting for transfers between devices: 11.3 us -> none  [on_device(): lax.all_to_all(expert_out.reshape(n_exp, capacity, expert_out.shape[1]),...]
    reduce_sum x6 -> x0, other arithmetic: 4.89 us -> none  [the longest x1 2.01 us: on_device(): total = jnp.sum(expd, axis=-1)]
  transfers between devices with their start and end apart: 5 -> 0, of which waited for: 5 -> 0; matrix products, arithmetic and copies ran while one was open for 2% -> 0% of each run, Pallas kernels for 0% -> 0%
where the time goes in v3:
time: 177 us; the launch traced here: 176 us
  Pallas kernels  173 us (98%)
  local copies, waits for them, and re-layouts  3.23 us (2%)
    pallas_call x1, Pallas kernels, on_device(): pl.pallas_call(layer_kernel, out_shape=(jax.ShapeDtypeStruct(stream.shape...  173 us

profile of v3, /device:TPU:1, one launch (start us, length us, event | category | flops | bytes accessed | tf_op | source)
XLA Modules:
  0.0 176.5 jit_solution(139335880039351818)
XLA Ops:
  0.6 172.6 %layer.1 = (bf16[16,6144]{1,0:T(8,128)(2,1)}, bf16[16,6144]{1,0:T(8,128)(2,1)}) custom-call(bf16[128,1024]{1,0:T(8,128)(2,1)} %q_ref.1, bf16[128,128]{1,0:T(8,128)(2,1)} %k_ref.1, bf16[128,128]{1,0:T(8,128)(2,1)} %v_ref.1, s32[32]{0:T(128)} %order_ref.1, bf16[1024,384]{1,0:T(8,128)(2,1)} %proj_ref.1, bf16[16,6144]{1,0:T(8,128)(2,1)} %stream_ref.1, ...), custom_call_target="tpu_custom_call" | custom-call | flops 17179869184 | bytes 14155776 | tf_op jit(solution)/shard_map/layer/pallas_call | solution.py:499
  173.2 1.6 copy.16
  174.8 1.6 copy.17

commit v4 on v3

--- a/solution.py
+++ b/solution.py
@@ -8,9 +8,12 @@
 HEAD = 128
 MESH = pl.DeviceIdType.MESH
 VMEM_LIMIT = 62 * 2**20
-WIDTHS = (384, 768, 768, 768, 384)
-NC = len(WIDTHS)
-STARTS = tuple(sum(WIDTHS[:c]) for c in range(NC))
+SPLITS = ((1024, 1024, 1024), (1024, 1024, 1024))
+UNITS = tuple(
+    (part, sum(split[:c]), width) for part, split in enumerate(SPLITS) for c, width in enumerate(split)
+)
+FIRST = len(SPLITS[0])
+NC = len(UNITS)
 BF16, F32 = jnp.bfloat16, jnp.float32
 
 
@@ -35,10 +38,10 @@
     pl.semaphore_wait(barrier, len(devices))
 
 
-def slot_match(meta, core):
+def slot_match(meta, core, exp):
     row = lax.broadcasted_iota(jnp.int32, (128, 128), 0)
     lane = lax.broadcasted_iota(jnp.int32, (128, 128), 1)
-    expert = f32(row // 16)
+    expert = f32(lax.rem(exp + row // 16, 8))
     first = (meta[0:1, :] == expert) & (lane < 16)
     second = (meta[1:2, :] == expert) & (lane < 16)
     named = jnp.where(first | second, 1.0, 0.0)
@@ -61,9 +64,9 @@
 def layer_kernel(
     q_ref, k_ref, v_ref, order_ref, proj_ref, stream_ref, gain_ref, ids_ref, mix_ref,
     gate_ref, up_ref, down_ref, att_ref, out_ref,
-    kv, kpos, bias, wcat, heads, proj, got_y, sums, half_sum, got_x, summed, blocks,
+    kv, kpos, bias, wcat, heads, proj, got_y, sums, half_sum, got_x, got_pair, pair_sum, summed, blocks,
     wgu, wd, meta, meta_sib, nrm, nsib, disp, rows, rows_sib, acc, hid, part,
-    got1, got2, got3, got4, got5, final, back, contrib, contrib_sib,
+    got1, got2, got3, got4, got5, final, back, contrib, contrib_sib, contrib_own,
     load_sem, pre_s, pre_r, kv_s, kv_r, w_s, w_r, h_s, h_r, y_s, y_r, x_s, x_r, b_s, b_r,
     disp_s, disp_r, ga_s, ga_r, sib_s, sib_r, hid_s, hid_r, rs_s, rs_r, back_s, back_r,
 ):
@@ -72,7 +75,7 @@
     z, xh, core = ctx // 4, lax.rem(ctx // 2, 2), lax.rem(ctx, 2)
     y, xl = exp // 2, lax.rem(exp, 2)
     up_z, down_z, far_z = lax.rem(z + 1, 4), lax.rem(z + 3, 4), lax.rem(z + 2, 4)
-    half = sum(WIDTHS)
+    half = sum(SPLITS[0])
 
     def dev(a, b, c=None, e=None):
         return (a * 4 + b * 2 + (core if c is None else c), exp if e is None else e)
@@ -139,8 +142,7 @@
         pltpu.make_async_copy(up_ref.at[0], wgu.at[:, pl.ds(384, 384)], load_sem.at[2]),
         pltpu.make_async_copy(down_ref.at[0, :, core_half], wd.at[core_cols], load_sem.at[3]),
     ]
-    for load in loads:
-        load.start()
+    loads[0].start()
     kv[core, xh, z, 0] = k_ref[...]
     kv[core, xh, z, 1] = v_ref[...]
     meta[...] = jnp.zeros_like(meta)
@@ -173,12 +175,12 @@
     row = lax.broadcasted_iota(jnp.int32, (128, 1), 0)
     qpos = jnp.where(row < 64, order_ref[2 * ctx], order_ref[2 * ctx + 1]) * 64 + lax.rem(row, 64)
     bias[...] = jnp.where(kpos[...] <= qpos, 0.0, -1e30)
-    match_own, weight_own = slot_match(meta[...], core)
+    match_own, weight_own = slot_match(meta[...], core, exp)
     for copy in column[:3]:
         copy.wait_recv()
     share_kv = [send(kv.at[core, xh], kv.at[core, xh], kv_s.at[7], kv_r.at[7], sib)]
     send_meta.wait_recv()
-    match_sib, weight_sib = slot_match(meta_sib[...], 1 - core)
+    match_sib, weight_sib = slot_match(meta_sib[...], 1 - core, exp)
     for copy in column[3:]:
         copy.wait_recv()
     share_kv.append(send(kv.at[core, 1 - xh], kv.at[core, 1 - xh], kv_s.at[8], kv_r.at[8], sib))
@@ -214,6 +216,8 @@
     for i in range(2):
         attend(i)
         moves.append([send_heads(i, k, z, pl.ds(0, 128), device) for k, device in enumerate((zp, zm))])
+    for load in loads[1:]:
+        load.start()
     send_down = send(down_ref.at[0, :, sib_half], wd.at[core_cols], pre_s.at[2], pre_r.at[2], sib)
     far_w = []
     for i in range(4):
@@ -234,6 +238,7 @@
     to_y = [None] * 4
     to_x = [None] * 4
     to_block = [None] * 4
+    x_first = (1, 3)
 
     def project(*turns):
         places = [order[t] for t in turns]
@@ -243,15 +248,33 @@
             product += dot(lhs, wcat[i * 512 : (i + 1) * 512, :])
         for n, (t, b) in enumerate(zip(turns, places)):
             proj[b] = product[n * 128 : (n + 1) * 128].astype(BF16).reshape(4, 2, 16, 1536)
+            if t in x_first:
+                to_x[t] = send(
+                    proj.at[b, :, 1 - xl], got_pair.at[b], x_s.at[t], x_r.at[t],
+                    dev(z, xh, None, y * 2 + 1 - xl),
+                )
+                continue
             to_y[t] = [
                 send(proj.at[b, c], got_y.at[b, y], y_s.at[t, j], y_r.at[t, j], dev(z, xh, None, c * 2 + xl))
                 for j, c in enumerate(columns)
             ]
             got_y[b, y] = proj[b, y]
 
-    def add_y(*turns):
+    def add_first(*turns):
         for t in turns:
             b = order[t]
+            if t in x_first:
+                to_x[t].wait_recv()
+                pair_sum[b] = (f32(proj[b, :, xl]) + f32(got_pair[b])).astype(BF16)
+                to_y[t] = [
+                    send(
+                        pair_sum.at[b, c], got_y.at[b, y, 0], y_s.at[t, j], y_r.at[t, j],
+                        dev(z, xh, None, c * 2 + xl),
+                    )
+                    for j, c in enumerate(columns)
+                ]
+                got_y[b, y, 0] = pair_sum[b, y]
+                continue
             for copy in to_y[t]:
                 copy.wait_recv()
             sums[b] = jnp.sum(f32(got_y[b]), axis=0)
@@ -260,11 +283,16 @@
                 half_sum.at[b], got_x.at[b], x_s.at[t], x_r.at[t], dev(z, xh, None, y * 2 + 1 - xl)
             )
 
-    def add_x(*turns):
+    def add_second(*turns):
         for t in turns:
             b = order[t]
-            to_x[t].wait_recv()
-            total = (sums[b, xl] + f32(got_x[b])).astype(BF16)
+            if t in x_first:
+                for copy in to_y[t]:
+                    copy.wait_recv()
+                total = jnp.sum(f32(got_y[b, :, 0]), axis=0).astype(BF16)
+            else:
+                to_x[t].wait_recv()
+                total = (sums[b, xl] + f32(got_x[b])).astype(BF16)
             if t == 0:
                 blocks[z] = total
             else:
@@ -275,16 +303,16 @@
 
     project(0)
     project(1, 2)
-    add_y(0)
+    add_first(0)
     for i in range(2):
         moves[i][2].wait_recv()
         moves[i][3].wait_recv()
     project(3)
-    add_x(0)
-    add_y(1, 2)
-    add_x(1, 2)
-    add_y(3)
-    add_x(3)
+    add_second(0)
+    add_first(1, 2)
+    add_second(1, 2)
+    add_first(3)
+    add_second(3)
     for copy in to_block[1:]:
         copy.wait_recv()
     square = jnp.zeros((16, 1), F32)
@@ -303,20 +331,27 @@
     shares = [[] for _ in range(NC)]
 
     def dispatch(c):
-        cols = pl.ds(STARTS[c], WIDTHS[c])
-        picked = dot(match_own, nrm[core, :, cols]) + dot(match_sib, nsib[:, cols])
-        disp[c][...] = picked.astype(BF16).reshape(8, 16, WIDTHS[c])
+        half_of, start, width = UNITS[c]
+        cols = pl.ds(start, width)
+        slots = slice(half_of * 64, half_of * 64 + 64)
+        picked = dot(match_own[slots], nrm[core, :, cols]) + dot(match_sib[slots], nsib[:, cols])
+        disp[c][...] = picked.astype(BF16).reshape(4, 16, width)
         dispatches[c] = [
-            send(disp[c].at[e], rows[c].at[own, exp], disp_s.at[c, j], disp_r.at[c, j], dev(z, xh, None, e))
-            for j, e in enumerate(peers)
+            send(
+                disp[c].at[j], rows[c].at[own, j], disp_s.at[c, j], disp_r.at[c, j],
+                dev(z, xh, None, lax.rem(exp + half_of * 4 + j, 8)),
+            )
+            for j in range(4)
+            if half_of * 4 + j > 0
         ]
-        rows[c][own, exp] = disp[c][exp]
+        if half_of == 0:
+            rows[c][own, 0] = disp[c][0]
 
     def row_view(c):
         def view(block, piece):
             if piece is None:
                 return rows[c].at[block]
-            return rows[c].at[block, pl.ds(piece * 4, 4)]
+            return rows[c].at[block, pl.ds(piece * 2, 2)]
 
         return view
 
@@ -346,40 +381,129 @@
         share(c, far_z)
 
     def term(source, c, base, i):
-        lhs = source[c][pl.ds(i * 2, 2)].reshape(256, WIDTHS[c])
-        return dot(lhs, wgu[pl.ds(pl.multiple_of(base + STARTS[c], 128), WIDTHS[c]), :])
+        _, start, width = UNITS[c]
+        lhs = source[c][pl.ds(i * 4, 4)].reshape(256, width)
+        return dot(lhs, wgu[pl.ds(pl.multiple_of(base + start, 128), width), :])
 
     def multiply_own(c):
         if c == 0:
             loads[1].wait()
             loads[2].wait()
+        half_of, start, _ = UNITS[c]
 
         def body(i, carry):
             value = term(rows, c, core * half, i)
-            acc[i] = value if c == 0 else acc[i] + value
+            acc[half_of, i] = value if start == 0 else acc[half_of, i] + value
             return carry
 
-        lax.fori_loop(0, 4, body, 0)
-
-    sent_hidden = []
+        lax.fori_loop(0, 2, body, 0)
+
+    sent_hidden = [[], []]
 
     def multiply_sib(c):
         for copy in shares[c]:
             copy.wait_recv()
+        half_of, start, width = UNITS[c]
 
         def body(i, carry):
-            acc[i] += term(rows_sib, c, (1 - core) * half, i)
+            acc[half_of, i] += term(rows_sib, c, (1 - core) * half, i)
             return carry
 
-        if c < NC - 1:
-            lax.fori_loop(0, 4, body, 0)
+        if start + width < half:
+            lax.fori_loop(0, 2, body, 0)
             return
-        for i in range(4):
-            value = acc[i] + term(rows_sib, c, (1 - core) * half, i)
+        for i in range(2):
+            value = acc[half_of, i] + term(rows_sib, c, (1 - core) * half, i)
             gate_part, up_part = value[:, :384], value[:, 384:]
-            hid[i, :, core_cols] = (gate_part / (1.0 + jnp.exp(-gate_part)) * up_part).astype(BF16)
-            view = hid.at[i, :, core_cols]
-            sent_hidden.append(send(view, view, hid_s.at[i], hid_r.at[i], sib))
+            hid[half_of, i, :, core_cols] = (gate_part / (1.0 + jnp.exp(-gate_part)) * up_part).astype(BF16)
+            view = hid.at[half_of, i, :, core_cols]
+            sent_hidden[half_of].append(
+                send(view, view, hid_s.at[half_of, i], hid_r.at[half_of, i], sib)
+            )
+
+    reduce = [[None] * 8 for _ in range(NC)]
+    returns = [None] * NC
+
+    def send_sum(c, k, src, dst, device):
+        reduce[c][k] = send(src, dst, rs_s.at[c, k], rs_r.at[c, k], device)
+
+    def reduce_a(c):
+        half_of, start, width = UNITS[c]
+
+        def body(i, carry):
+            out = dot(hid[half_of, i], wd[:, start : start + width])
+            part[c][pl.ds(i * 4, 4)] = out.astype(BF16).reshape(4, 4, 16, width)
+            return carry
+
+        if c == 0:
+            loads[3].wait()
+            send_down.wait_recv()
+        if start == 0:
+            for i in range(2):
+                sent_hidden[half_of][i].wait_recv()
+                body(i, 0)
+        else:
+            lax.fori_loop(0, 2, body, 0)
+        send_sum(c, 0, part[c].at[blk(up_z, 1 - xh)], got1[c].at[0], zp)
+        send_sum(c, 1, part[c].at[blk(down_z, 1 - xh)], got1[c].at[1], zm)
+        send_sum(c, 2, part[c].at[blk(far_z, 1 - xh)], got2[c], xp)
+
+    def reduce_b(c):
+        reduce[c][2].wait_recv()
+        block = blk(far_z, xh)
+        part[c][block] = (f32(part[c][block]) + f32(got2[c][...])).astype(BF16)
+        send_sum(c, 3, part[c].at[block, pl.ds(0, 2)], got4[c].at[0], zm)
+        send_sum(c, 4, part[c].at[block, pl.ds(2, 2)], got4[c].at[1], zp)
+        reduce[c][0].wait_recv()
+        reduce[c][1].wait_recv()
+        block = blk(z, 1 - xh)
+        part[c][block] = (f32(part[c][block]) + f32(got1[c][0]) + f32(got1[c][1])).astype(BF16)
+        send_sum(c, 5, part[c].at[block], got3[c], xp)
+
+    def reduce_c(c):
+        reduce[c][3].wait_recv()
+        block = blk(down_z, xh)
+        part[c][block, 0:2] = (f32(part[c][block, 0:2]) + f32(got4[c][0])).astype(BF16)
+        send_sum(c, 6, part[c].at[block], got5[c].at[0], zm)
+        reduce[c][4].wait_recv()
+        block = blk(up_z, xh)
+        part[c][block, 2:4] = (f32(part[c][block, 2:4]) + f32(got4[c][1])).astype(BF16)
+        send_sum(c, 7, part[c].at[block], got5[c].at[1], zp)
+
+    def reduce_d(c):
+        for k in (5, 6, 7):
+            reduce[c][k].wait_recv()
+        final[c][...] = (f32(part[c][own]) + f32(got3[c][...]) + (f32(got5[c][0]) + f32(got5[c][1]))).astype(BF16)
+        half_of = UNITS[c][0]
+        returns[c] = [
+            send(
+                final[c].at[j], back[c].at[j], back_s.at[c, j], back_r.at[c, j],
+                dev(z, xh, None, lax.rem(exp + 8 - half_of * 4 - j, 8)),
+            )
+            for j in range(4)
+            if half_of * 4 + j > 0
+        ]
+        if half_of == 0:
+            back[c][0] = final[c][0]
+
+    def weigh(weight, values):
+        return jnp.dot(weight, values, precision=lax.Precision.HIGHEST, preferred_element_type=F32)
+
+    def combine(c):
+        for copy in returns[c]:
+            copy.wait_recv()
+        half_of, start, width = UNITS[c]
+        values = f32(back[c][...].reshape(64, width))
+        slots = slice(half_of * 64, half_of * 64 + 64)
+        for_sib, for_own = weigh(weight_sib[:, slots], values), weigh(weight_own[:, slots], values)
+        cols = slice(start, start + width)
+        if half_of == 0:
+            contrib_sib[:, cols] = for_sib
+            contrib_own[:, cols] = for_own
+            return
+        contrib_sib[:, cols] += for_sib
+        place = pl.ds(pl.multiple_of(core * half + start, 128), width)
+        out_ref[:, place] = (f32(att_ref[:, place]) + (contrib_own[:, cols] + for_own)).astype(BF16)
 
     dispatch(0)
     dispatch(1)
@@ -392,76 +516,12 @@
         (3, gather_d),
         (3, multiply_own),
         (4, multiply_sib),
+        (FIRST + 3, reduce_a),
+        (FIRST + 4, reduce_b),
+        (FIRST + 5, reduce_c),
+        (FIRST + 6, reduce_d),
+        (FIRST + 7, combine),
     )
-    loads[3].wait()
-    send_down.wait_recv()
-
-    reduce = [[None] * 8 for _ in range(NC)]
-    returns = [None] * NC
-
-    def send_sum(c, k, src, dst, device):
-        reduce[c][k] = send(src, dst, rs_s.at[c, k], rs_r.at[c, k], device)
-
-    def reduce_a(c):
-        def body(i, carry):
-            out = dot(hid[i], wd[:, STARTS[c] : STARTS[c] + WIDTHS[c]])
-            part[c][pl.ds(i * 2, 2)] = out.astype(BF16).reshape(2, 8, 16, WIDTHS[c])
-            return carry
-
-        if c == 0:
-            for i in range(4):
-                sent_hidden[i].wait_recv()
-                body(i, 0)
-        else:
-            lax.fori_loop(0, 4, body, 0)
-        send_sum(c, 0, part[c].at[blk(up_z, 1 - xh)], got1[c].at[0], zp)
-        send_sum(c, 1, part[c].at[blk(down_z, 1 - xh)], got1[c].at[1], zm)
-        send_sum(c, 2, part[c].at[blk(far_z, 1 - xh)], got2[c], xp)
-
-    def reduce_b(c):
-        reduce[c][2].wait_recv()
-        block = blk(far_z, xh)
-        part[c][block] = (f32(part[c][block]) + f32(got2[c][...])).astype(BF16)
-        send_sum(c, 3, part[c].at[block, pl.ds(0, 4)], got4[c].at[0], zm)
-        send_sum(c, 4, part[c].at[block, pl.ds(4, 4)], got4[c].at[1], zp)
-        reduce[c][0].wait_recv()
-        reduce[c][1].wait_recv()
-        block = blk(z, 1 - xh)
-        part[c][block] = (f32(part[c][block]) + f32(got1[c][0]) + f32(got1[c][1])).astype(BF16)
-        send_sum(c, 5, part[c].at[block], got3[c], xp)
-
-    def reduce_c(c):
-        reduce[c][3].wait_recv()
-        block = blk(down_z, xh)
-        part[c][block, 0:4] = (f32(part[c][block, 0:4]) + f32(got4[c][0])).astype(BF16)
-        send_sum(c, 6, part[c].at[block], got5[c].at[0], zm)
-        reduce[c][4].wait_recv()
-        block = blk(up_z, xh)
-        part[c][block, 4:8] = (f32(part[c][block, 4:8]) + f32(got4[c][1])).astype(BF16)
-        send_sum(c, 7, part[c].at[block], got5[c].at[1], zp)
-
-    def reduce_d(c):
-        for k in (5, 6, 7):
-            reduce[c][k].wait_recv()
-        final[c][...] = (f32(part[c][own]) + f32(got3[c][...]) + (f32(got5[c][0]) + f32(got5[c][1]))).astype(BF16)
-        returns[c] = [
-            send(final[c].at[e], back[c].at[exp], back_s.at[c, j], back_r.at[c, j], dev(z, xh, None, e))
-            for j, e in enumerate(peers)
-        ]
-        back[c][exp] = final[c][exp]
-
-    def weigh(weight, values):
-        return jnp.dot(weight, values, precision=lax.Precision.HIGHEST, preferred_element_type=F32)
-
-    def combine(c):
-        for copy in returns[c]:
-            copy.wait_recv()
-        values = f32(back[c][...].reshape(128, WIDTHS[c]))
-        contrib_sib[:, STARTS[c] : STARTS[c] + WIDTHS[c]] = weigh(weight_sib, values)
-        cols = pl.ds(pl.multiple_of(core * half + STARTS[c], 128), WIDTHS[c])
-        out_ref[:, cols] = (f32(att_ref[:, cols]) + weigh(weight_own, values)).astype(BF16)
-
-    staged(NC, (0, reduce_a), (1, reduce_b), (2, reduce_c), (3, reduce_d), (4, combine))
 
     last = send(contrib_sib, contrib, pre_s.at[4], pre_r.at[4], sib)
     last.wait_recv()
@@ -491,7 +551,7 @@
     anyspace = pl.BlockSpec(memory_space=pl.ANY)
 
     def per_chunk(*shape):
-        return [pltpu.VMEM(shape + (width,), BF16) for width in WIDTHS]
+        return [pltpu.VMEM(shape + (width,), BF16) for _, _, width in UNITS]
 
     def sems(*shapes):
         return [pltpu.SemaphoreType.DMA(shape) for shape in shapes for _ in range(2)]
@@ -512,6 +572,8 @@
             pltpu.VMEM((4, 2, 16, 1536), F32),
             pltpu.VMEM((4, 16, 1536), BF16),
             pltpu.VMEM((4, 16, 1536), BF16),
+            pltpu.VMEM((4, 4, 16, 1536), BF16),
+            pltpu.VMEM((4, 4, 16, 1536), BF16),
             pltpu.VMEM((4, 16, 1536), BF16),
             pltpu.VMEM((4, 16, 1536), BF16),
             pltpu.VMEM((d, 768), BF16),
@@ -520,26 +582,27 @@
             pltpu.VMEM((8, 128), F32),
             pltpu.VMEM((2, 16, half), BF16),
             pltpu.VMEM((16, half), BF16),
-            per_chunk(8, 16),
-            per_chunk(8, 8, 16),
-            per_chunk(8, 8, 16),
-            pltpu.VMEM((4, 256, 768), F32),
-            pltpu.VMEM((4, 256, 768), BF16),
-            per_chunk(8, 8, 16),
-            per_chunk(2, 8, 16),
-            per_chunk(8, 16),
-            per_chunk(8, 16),
+            per_chunk(4, 16),
+            per_chunk(8, 4, 16),
+            per_chunk(8, 4, 16),
+            pltpu.VMEM((2, 2, 256, 768), F32),
+            pltpu.VMEM((2, 2, 256, 768), BF16),
+            per_chunk(8, 4, 16),
             per_chunk(2, 4, 16),
-            per_chunk(2, 8, 16),
-            per_chunk(8, 16),
-            per_chunk(8, 16),
+            per_chunk(4, 16),
+            per_chunk(4, 16),
+            per_chunk(2, 2, 16),
+            per_chunk(2, 4, 16),
+            per_chunk(4, 16),
+            per_chunk(4, 16),
+            pltpu.VMEM((16, half), F32),
             pltpu.VMEM((16, half), F32),
             pltpu.VMEM((16, half), F32),
             pltpu.SemaphoreType.DMA((4,)),
         ]
         + sems(
             (5,), (9,), (8,), (2, 4), (4, 3), (4,), (3,),
-            (NC, 7), (NC, 8), (NC, 4), (4,), (NC, 8), (NC, 7),
+            (NC, 4), (NC, 8), (NC, 4), (2, 2), (NC, 8), (NC, 4),
         ),
         compiler_params=pltpu.CompilerParams(
             collective_id=0, has_side_effects=True, vmem_limit_bytes=VMEM_LIMIT

time: 177 us -> 168 us (0.949)
  Pallas kernels: 173 us -> 164 us
    pallas_call x1, Pallas kernels: 173 us -> 164 us  [on_device(): pl.pallas_call(layer_kernel, out_shape=(jax.ShapeDtypeStruct(stream.shape...]
where the time goes in v4:
time: 168 us
  Pallas kernels  164 us (98%)
  local copies, waits for them, and re-layouts  3.23 us (2%)
    pallas_call x1, Pallas kernels, on_device(): pl.pallas_call(layer_kernel, out_shape=(jax.ShapeDtypeStruct(stream.shape...  164 us

profile of v4, /device:TPU:1, one launch (start us, length us, event | category | flops | bytes accessed | tf_op | source)
XLA Modules:
  0.0 167.9 jit_solution(11931452410962165272)
XLA Ops:
  0.6 164.0 %layer.1 = (bf16[16,6144]{1,0:T(8,128)(2,1)}, bf16[16,6144]{1,0:T(8,128)(2,1)}) custom-call(bf16[128,1024]{1,0:T(8,128)(2,1)} %q_ref.1, bf16[128,128]{1,0:T(8,128)(2,1)} %k_ref.1, bf16[128,128]{1,0:T(8,128)(2,1)} %v_ref.1, s32[32]{0:T(128)} %order_ref.1, bf16[1024,384]{1,0:T(8,128)(2,1)} %proj_ref.1, bf16[16,6144]{1,0:T(8,128)(2,1)} %stream_ref.1, ...), custom_call_target="tpu_custom_call" | custom-call | flops 17179869184 | bytes 14155776 | tf_op jit(solution)/shard_map/layer/pallas_call | solution.py:559
  164.7 1.6 copy.16
  166.3 1.6 copy.17

commit v5 on v4

--- a/solution.py
+++ b/solution.py
@@ -8,7 +8,7 @@
 HEAD = 128
 MESH = pl.DeviceIdType.MESH
 VMEM_LIMIT = 62 * 2**20
-SPLITS = ((1024, 1024, 1024), (1024, 1024, 1024))
+SPLITS = ((768, 768, 768, 768), (768, 768, 768, 768))
 UNITS = tuple(
     (part, sum(split[:c]), width) for part, split in enumerate(SPLITS) for c, width in enumerate(split)
 )
@@ -219,6 +219,79 @@
     for load in loads[1:]:
         load.start()
     send_down = send(down_ref.at[0, :, sib_half], wd.at[core_cols], pre_s.at[2], pre_r.at[2], sib)
+    loads[0].wait()
+    send_w_sib.wait_recv()
+
+    order = [(h, a) for h in (xh, 1 - xh) for a in (z, down_z, up_z, far_z)]
+    to_y = [None] * 8
+    to_x = [None] * 8
+    to_block = [None] * 8
+    x_first = (2, 3, 5, 6)
+
+    def project(*turns):
+        side = order[turns[0]][0]
+        side_cols = pl.ds(pl.multiple_of(side * 768, 128), 768)
+        product = 0.0
+        for i in range(2):
+            lhs = jnp.concatenate([heads[i, order[t][1]] for t in turns], axis=0)
+            product += dot(lhs, wcat[i * 512 : (i + 1) * 512, side_cols])
+        for n, t in enumerate(turns):
+            b = order[t]
+            proj[*b] = product[n * 128 : (n + 1) * 128].astype(BF16).reshape(4, 2, 16, 768)
+            if t in x_first:
+                to_x[t] = send(
+                    proj.at[*b, :, 1 - xl], got_pair.at[*b], x_s.at[t], x_r.at[t],
+                    dev(z, xh, None, y * 2 + 1 - xl),
+                )
+                continue
+            to_y[t] = [
+                send(proj.at[*b, c], got_y.at[*b, y], y_s.at[t, j], y_r.at[t, j], dev(z, xh, None, c * 2 + xl))
+                for j, c in enumerate(columns)
+            ]
+            got_y[*b, y] = proj[*b, y]
+
+    def add_first(*turns):
+        for t in turns:
+            b = order[t]
+            if t in x_first:
+                to_x[t].wait_recv()
+                pair_sum[*b] = (f32(proj[*b, :, xl]) + f32(got_pair[*b])).astype(BF16)
+                to_y[t] = [
+                    send(
+                        pair_sum.at[*b, c], got_y.at[*b, y, 0], y_s.at[t, j], y_r.at[t, j],
+                        dev(z, xh, None, c * 2 + xl),
+                    )
+                    for j, c in enumerate(columns)
+                ]
+                got_y[*b, y, 0] = pair_sum[*b, y]
+                continue
+            for copy in to_y[t]:
+                copy.wait_recv()
+            sums[*b] = jnp.sum(f32(got_y[*b]), axis=0)
+            half_sum[*b] = sums[*b, 1 - xl].astype(BF16)
+            to_x[t] = send(
+                half_sum.at[*b], got_x.at[*b], x_s.at[t], x_r.at[t], dev(z, xh, None, y * 2 + 1 - xl)
+            )
+
+    def add_second(*turns):
+        for t in turns:
+            b = order[t]
+            if t in x_first:
+                for copy in to_y[t]:
+                    copy.wait_recv()
+                total = jnp.sum(f32(got_y[*b, :, 0]), axis=0).astype(BF16)
+            else:
+                to_x[t].wait_recv()
+                total = (sums[*b, xl] + f32(got_x[*b])).astype(BF16)
+            if t % 4 == 0:
+                blocks[b[0], z] = total
+            else:
+                summed[*b] = total
+                to_block[t] = send(
+                    summed.at[*b], blocks.at[b[0], z], b_s.at[t], b_r.at[t], dev(b[1], xh)
+                )
+
+    project(0)
     far_w = []
     for i in range(4):
         send_w[i].wait_recv()
@@ -229,96 +302,30 @@
         moves[i].append(send_heads(i, 2, down_z, pl.ds(0, 64), zp))
         moves[i][1].wait_recv()
         moves[i].append(send_heads(i, 3, up_z, pl.ds(64, 64), zm))
-    loads[0].wait()
-    send_w_sib.wait_recv()
+    project(1, 2)
     for copy in far_w:
         copy.wait_recv()
-
-    order = [z, down_z, up_z, far_z]
-    to_y = [None] * 4
-    to_x = [None] * 4
-    to_block = [None] * 4
-    x_first = (1, 3)
-
-    def project(*turns):
-        places = [order[t] for t in turns]
-        product = 0.0
-        for i in range(2):
-            lhs = jnp.concatenate([heads[i, b] for b in places], axis=0)
-            product += dot(lhs, wcat[i * 512 : (i + 1) * 512, :])
-        for n, (t, b) in enumerate(zip(turns, places)):
-            proj[b] = product[n * 128 : (n + 1) * 128].astype(BF16).reshape(4, 2, 16, 1536)
-            if t in x_first:
-                to_x[t] = send(
-                    proj.at[b, :, 1 - xl], got_pair.at[b], x_s.at[t], x_r.at[t],
-                    dev(z, xh, None, y * 2 + 1 - xl),
-                )
-                continue
-            to_y[t] = [
-                send(proj.at[b, c], got_y.at[b, y], y_s.at[t, j], y_r.at[t, j], dev(z, xh, None, c * 2 + xl))
-                for j, c in enumerate(columns)
-            ]
-            got_y[b, y] = proj[b, y]
-
-    def add_first(*turns):
-        for t in turns:
-            b = order[t]
-            if t in x_first:
-                to_x[t].wait_recv()
-                pair_sum[b] = (f32(proj[b, :, xl]) + f32(got_pair[b])).astype(BF16)
-                to_y[t] = [
-                    send(
-                        pair_sum.at[b, c], got_y.at[b, y, 0], y_s.at[t, j], y_r.at[t, j],
-                        dev(z, xh, None, c * 2 + xl),
-                    )
-                    for j, c in enumerate(columns)
-                ]
-                got_y[b, y, 0] = pair_sum[b, y]
-                continue
-            for copy in to_y[t]:
-                copy.wait_recv()
-            sums[b] = jnp.sum(f32(got_y[b]), axis=0)
-            half_sum[b] = sums[b, 1 - xl].astype(BF16)
-            to_x[t] = send(
-                half_sum.at[b], got_x.at[b], x_s.at[t], x_r.at[t], dev(z, xh, None, y * 2 + 1 - xl)
-            )
-
-    def add_second(*turns):
-        for t in turns:
-            b = order[t]
-            if t in x_first:
-                for copy in to_y[t]:
-                    copy.wait_recv()
-                total = jnp.sum(f32(got_y[b, :, 0]), axis=0).astype(BF16)
-            else:
-                to_x[t].wait_recv()
-                total = (sums[b, xl] + f32(got_x[b])).astype(BF16)
-            if t == 0:
-                blocks[z] = total
-            else:
-                summed[b] = total
-                to_block[t] = send(
-                    summed.at[b], blocks.at[z], b_s.at[t - 1], b_r.at[t - 1], dev(b, xh)
-                )
-
-    project(0)
-    project(1, 2)
-    add_first(0)
+    project(4, 5, 6)
+    add_first(0, 1, 2)
     for i in range(2):
         moves[i][2].wait_recv()
         moves[i][3].wait_recv()
     project(3)
-    add_second(0)
-    add_first(1, 2)
-    add_second(1, 2)
-    add_first(3)
-    add_second(3)
-    for copy in to_block[1:]:
-        copy.wait_recv()
+    project(7)
+    add_second(0, 1)
+    add_first(4, 5)
+    add_second(2)
+    add_first(6, 3)
+    add_second(4, 5)
+    add_first(7)
+    add_second(6, 3, 7)
+    for copy in to_block:
+        if copy is not None:
+            copy.wait_recv()
     square = jnp.zeros((16, 1), F32)
-    for b in range(4):
-        cols = slice(b * 1536, (b + 1) * 1536)
-        attended = (f32(stream_ref[:, cols]) + f32(blocks[b])).astype(BF16)
+    for b in range(8):
+        cols = slice(b * 768, (b + 1) * 768)
+        attended = (f32(stream_ref[:, cols]) + f32(blocks[b % 2, b // 2])).astype(BF16)
         att_ref[:, cols] = attended
         square += jnp.sum(f32(attended) * f32(attended), axis=-1, keepdims=True)
     normed = f32(att_ref[...]) * lax.rsqrt(square / (2 * half) + 1e-05) * gain_ref[...]
@@ -567,15 +574,15 @@
             pltpu.VMEM((128, 2048), F32),
             pltpu.VMEM((1024, 1536), BF16),
             pltpu.VMEM((2, 4, 128, 512), BF16),
-            pltpu.VMEM((4, 4, 2, 16, 1536), BF16),
-            pltpu.VMEM((4, 4, 2, 16, 1536), BF16),
-            pltpu.VMEM((4, 2, 16, 1536), F32),
-            pltpu.VMEM((4, 16, 1536), BF16),
-            pltpu.VMEM((4, 16, 1536), BF16),
-            pltpu.VMEM((4, 4, 16, 1536), BF16),
-            pltpu.VMEM((4, 4, 16, 1536), BF16),
-            pltpu.VMEM((4, 16, 1536), BF16),
-            pltpu.VMEM((4, 16, 1536), BF16),
+            pltpu.VMEM((2, 4, 4, 2, 16, 768), BF16),
+            pltpu.VMEM((2, 4, 4, 2, 16, 768), BF16),
+            pltpu.VMEM((2, 4, 2, 16, 768), F32),
+            pltpu.VMEM((2, 4, 16, 768), BF16),
+            pltpu.VMEM((2, 4, 16, 768), BF16),
+            pltpu.VMEM((2, 4, 4, 16, 768), BF16),
+            pltpu.VMEM((2, 4, 4, 16, 768), BF16),
+            pltpu.VMEM((2, 4, 16, 768), BF16),
+            pltpu.VMEM((2, 4, 16, 768), BF16),
             pltpu.VMEM((d, 768), BF16),
             pltpu.VMEM((768, half), BF16),
             pltpu.VMEM((8, 128), F32),
@@ -601,7 +608,7 @@
             pltpu.SemaphoreType.DMA((4,)),
         ]
         + sems(
-            (5,), (9,), (8,), (2, 4), (4, 3), (4,), (3,),
+            (5,), (9,), (8,), (2, 4), (8, 3), (8,), (8,),
             (NC, 4), (NC, 8), (NC, 4), (2, 2), (NC, 8), (NC, 4),
         ),
         compiler_params=pltpu.CompilerParams(

time: 168 us -> 162 us (0.964)
  Pallas kernels: 164 us -> 158 us
    pallas_call x1, Pallas kernels: 164 us -> 158 us  [on_device(): pl.pallas_call(layer_kernel, out_shape=(jax.ShapeDtypeStruct(stream.shape...]
where the time goes in v5:
time: 162 us; the launch traced here: 161 us
  Pallas kernels  158 us (98%)
  local copies, waits for them, and re-layouts  3.23 us (2%)
    pallas_call x1, Pallas kernels, on_device(): pl.pallas_call(layer_kernel, out_shape=(jax.ShapeDtypeStruct(stream.shape...  158 us

profile of v5, /device:TPU:1, one launch (start us, length us, event | category | flops | bytes accessed | tf_op | source)
XLA Modules:
  0.0 161.5 jit_solution(7700218181865488979)
XLA Ops:
  0.6 157.6 %layer.1 = (bf16[16,6144]{1,0:T(8,128)(2,1)}, bf16[16,6144]{1,0:T(8,128)(2,1)}) custom-call(bf16[128,1024]{1,0:T(8,128)(2,1)} %q_ref.1, bf16[128,128]{1,0:T(8,128)(2,1)} %k_ref.1, bf16[128,128]{1,0:T(8,128)(2,1)} %v_ref.1, s32[32]{0:T(128)} %order_ref.1, bf16[1024,384]{1,0:T(8,128)(2,1)} %proj_ref.1, bf16[16,6144]{1,0:T(8,128)(2,1)} %stream_ref.1, ...), custom_call_target="tpu_custom_call" | custom-call | flops 17179869184 | bytes 14155776 | tf_op jit(solution)/shard_map/layer/pallas_call | solution.py:566
  158.2 1.6 %copy.16 = bf16[16,6144]{1,0:T(8,128)(2,1)} copy(bf16[16,6144]{1,0:T(8,128)(2,1)} %get-tuple-element.4) | data formatting | bytes 393216
  159.8 1.6 %copy.17 = bf16[16,6144]{1,0:T(8,128)(2,1)} copy(bf16[16,6144]{1,0:T(8,128)(2,1)} %get-tuple-element.5) | data formatting | bytes 393216

commit v6 on v5

--- a/solution.py
+++ b/solution.py
@@ -68,7 +68,7 @@
     wgu, wd, meta, meta_sib, nrm, nsib, disp, rows, rows_sib, acc, hid, part,
     got1, got2, got3, got4, got5, final, back, contrib, contrib_sib, contrib_own,
     load_sem, pre_s, pre_r, kv_s, kv_r, w_s, w_r, h_s, h_r, y_s, y_r, x_s, x_r, b_s, b_r,
-    disp_s, disp_r, ga_s, ga_r, sib_s, sib_r, hid_s, hid_r, rs_s, rs_r, back_s, back_r,
+    disp_s, disp_r, ga_s, ga_r, sib_s, sib_r, hid_s, hid_r, rs_s, rs_r, back_s, back_r, last_s, last_r,
 ):
     ctx = lax.axis_index("ctx")
     exp = lax.axis_index("exp")
@@ -392,35 +392,28 @@
         lhs = source[c][pl.ds(i * 4, 4)].reshape(256, width)
         return dot(lhs, wgu[pl.ds(pl.multiple_of(base + start, 128), width), :])
 
-    def multiply_own(c):
+    sent_hidden = [[], []]
+
+    def both(c, i):
+        return term(rows, c, core * half, i) + term(rows_sib, c, (1 - core) * half, i)
+
+    def multiply(c):
         if c == 0:
             loads[1].wait()
             loads[2].wait()
-        half_of, start, _ = UNITS[c]
-
-        def body(i, carry):
-            value = term(rows, c, core * half, i)
-            acc[half_of, i] = value if start == 0 else acc[half_of, i] + value
-            return carry
-
-        lax.fori_loop(0, 2, body, 0)
-
-    sent_hidden = [[], []]
-
-    def multiply_sib(c):
         for copy in shares[c]:
             copy.wait_recv()
         half_of, start, width = UNITS[c]
 
         def body(i, carry):
-            acc[half_of, i] += term(rows_sib, c, (1 - core) * half, i)
+            acc[half_of, i] = both(c, i) if start == 0 else acc[half_of, i] + both(c, i)
             return carry
 
         if start + width < half:
             lax.fori_loop(0, 2, body, 0)
             return
         for i in range(2):
-            value = acc[half_of, i] + term(rows_sib, c, (1 - core) * half, i)
+            value = acc[half_of, i] + both(c, i)
             gate_part, up_part = value[:, :384], value[:, 384:]
             hid[half_of, i, :, core_cols] = (gate_part / (1.0 + jnp.exp(-gate_part)) * up_part).astype(BF16)
             view = hid.at[half_of, i, :, core_cols]
@@ -496,6 +489,8 @@
     def weigh(weight, values):
         return jnp.dot(weight, values, precision=lax.Precision.HIGHEST, preferred_element_type=F32)
 
+    lasts = []
+
     def combine(c):
         for copy in returns[c]:
             copy.wait_recv()
@@ -509,8 +504,19 @@
             contrib_own[:, cols] = for_own
             return
         contrib_sib[:, cols] += for_sib
+        n = c - FIRST
+        view = pl.ds(start, width)
+        lasts.append(send(contrib_sib.at[:, view], contrib.at[:, view], last_s.at[n], last_r.at[n], sib))
         place = pl.ds(pl.multiple_of(core * half + start, 128), width)
         out_ref[:, place] = (f32(att_ref[:, place]) + (contrib_own[:, cols] + for_own)).astype(BF16)
+
+    def finish(c):
+        if c < FIRST:
+            return
+        lasts[c - FIRST].wait_recv()
+        _, start, width = UNITS[c]
+        place = pl.ds(pl.multiple_of((1 - core) * half + start, 128), width)
+        out_ref[:, place] = (f32(att_ref[:, place]) + contrib[:, start : start + width]).astype(BF16)
 
     dispatch(0)
     dispatch(1)
@@ -521,18 +527,15 @@
         (1, gather_b),
         (2, gather_c),
         (3, gather_d),
-        (3, multiply_own),
-        (4, multiply_sib),
+        (4, multiply),
         (FIRST + 3, reduce_a),
         (FIRST + 4, reduce_b),
         (FIRST + 5, reduce_c),
         (FIRST + 6, reduce_d),
         (FIRST + 7, combine),
+        (FIRST + 8, finish),
     )
 
-    last = send(contrib_sib, contrib, pre_s.at[4], pre_r.at[4], sib)
-    last.wait_recv()
-    out_ref[:, sib_half] = (f32(att_ref[:, sib_half]) + contrib[...]).astype(BF16)
     for copy in started:
         copy.wait_send()
 
@@ -609,7 +612,7 @@
         ]
         + sems(
             (5,), (9,), (8,), (2, 4), (8, 3), (8,), (8,),
-            (NC, 4), (NC, 8), (NC, 4), (2, 2), (NC, 8), (NC, 4),
+            (NC, 4), (NC, 8), (NC, 4), (2, 2), (NC, 8), (NC, 4), (NC - FIRST,),
         ),
         compiler_params=pltpu.CompilerParams(
             collective_id=0, has_side_effects=True, vmem_limit_bytes=VMEM_LIMIT

time: 162 us -> 162 us (level)
  no operation moved by 1% of the time
where the time goes in v6:
time: 162 us; the launch traced here: 161 us
  Pallas kernels  158 us (98%)
  local copies, waits for them, and re-layouts  3.23 us (2%)
    pallas_call x1, Pallas kernels, on_device(): pl.pallas_call(layer_kernel, out_shape=(jax.ShapeDtypeStruct(stream.shape...  158 us

profile of v6, /device:TPU:1, one launch (start us, length us, event | category | flops | bytes accessed | tf_op | source)
XLA Modules:
  0.0 161.4 jit_solution(11955964178867993238)
XLA Ops:
  0.6 157.5 %layer.1 = (bf16[16,6144]{1,0:T(8,128)(2,1)}, bf16[16,6144]{1,0:T(8,128)(2,1)}) custom-call(bf16[128,1024]{1,0:T(8,128)(2,1)} %q_ref.1, bf16[128,128]{1,0:T(8,128)(2,1)} %k_ref.1, bf16[128,128]{1,0:T(8,128)(2,1)} %v_ref.1, s32[32]{0:T(128)} %order_ref.1, bf16[1024,384]{1,0:T(8,128)(2,1)} %proj_ref.1, bf16[16,6144]{1,0:T(8,128)(2,1)} %stream_ref.1, ...), custom_call_target="tpu_custom_call" | custom-call | flops 17179869184 | bytes 14155776 | tf_op jit(solution)/shard_map/layer/pallas_call | solution.py:569
  158.2 1.6 %copy.16 = bf16[16,6144]{1,0:T(8,128)(2,1)} copy(bf16[16,6144]{1,0:T(8,128)(2,1)} %get-tuple-element.4) | data formatting | bytes 393216
  159.8 1.6 %copy.17 = bf16[16,6144]{1,0:T(8,128)(2,1)} copy(bf16[16,6144]{1,0:T(8,128)(2,1)} %get-tuple-element.5) | data formatting | bytes 393216
